TPU v7x, 512 devices: a whole 4x8x8 slice. The times are simulated.
512 devices in a mesh: uly: 8 (over x, z_lo), blk: 64 (over y, z_hi, core).
Axes of the slice: x: 4, y: 8, z: 8 (z_hi: 4, z_lo: 2; z = z_hi * 2 + z_lo), core: 2. Of those that a mesh axis runs over, the one named last changes fastest.
Arguments:
- queries: bfloat16 [16384, 3072], P(('uly', 'blk')), may hold values from -8 to 8
- keys: bfloat16 [16384, 3072], P(('uly', 'blk')), may hold values from -8 to 8
- values: bfloat16 [16384, 3072], P(('uly', 'blk')), may hold values from -6 to 6
Outputs:
- attended: bfloat16 [16384, 3072], P(('uly', 'blk'))
All inputs are finite; a program needn't handle non-finite values.
Results may differ from a plain program's by a relative error of at most 0.025.
Values may be sent and summed in bfloat16 or wider, within the bound.
No kernel may reach another device: no remote copies, remote signals or barrier semaphores. Data moves between devices by JAX's collectives and lax.ppermute only.
A program may use at most 64 MiB of HBM per device.

v0:
```python
import math

import jax
import jax.numpy as jnp
from jax import lax
from jax.sharding import PartitionSpec as P

HEAD_DIM = 128


def combine_parts(first, second):
    best_a, total_a, running_a = first
    best_b, total_b, running_b = second
    new_best = jnp.maximum(best_a, best_b)
    factor_a = jnp.exp(best_a - new_best)
    factor_b = jnp.exp(best_b - new_best)
    total = total_a * factor_a + total_b * factor_b
    running = running_a * factor_a[..., None] + running_b * factor_b[..., None]
    return (new_best, total, running)


def tile_parts(q_rows, key_rows, value_rows, scale):
    row_count, head_count, head_size = q_rows.shape
    block = math.gcd(row_count, 512)
    q_blocks = q_rows.reshape(row_count // block, block, head_count, head_size)

    def one_block(q_block):
        scores = (
            jnp.einsum("qhd,khd->qhk", q_block, key_rows, preferred_element_type=jnp.float32)
            * scale
        )
        best = jnp.max(scores, axis=2)
        expo_vals = jnp.exp(scores - best[..., None])
        total = jnp.sum(expo_vals, axis=2)
        running = jnp.einsum(
            "qhk,khd->qhd",
            expo_vals.astype(jnp.bfloat16),
            value_rows,
            preferred_element_type=jnp.float32,
        )
        return (best, total, running)

    best, total, running = lax.map(one_block, q_blocks)
    return (
        best.reshape(row_count, head_count),
        total.reshape(row_count, head_count),
        running.reshape(row_count, head_count, head_size),
    )


def cycle_plan(q_local, k_local, v_local, scale):
    row_count, head_count, head_size = q_local.shape
    initial = (
        jnp.full((row_count, head_count), -1e30, jnp.float32),
        jnp.zeros((row_count, head_count), jnp.float32),
        jnp.zeros((row_count, head_count, head_size), jnp.float32),
    )
    carry = initial
    key_piece = lax.all_gather(k_local, "blk", axis=0, tiled=True)
    value_piece = lax.all_gather(v_local, "blk", axis=0, tiled=True)
    piece_rows = key_piece.shape[0]
    step_rows = math.gcd(piece_rows, 1536)
    key_blocks = key_piece.reshape(piece_rows // step_rows, step_rows, head_count, head_size)
    value_blocks = value_piece.reshape(piece_rows // step_rows, step_rows, head_count, head_size)

    def one_step(state, pair):
        part = tile_parts(q_local, pair[0], pair[1], scale)
        return (combine_parts(state, part), None)

    carry, unused = lax.scan(one_step, carry, (key_blocks, value_blocks))
    return carry


def shards(queries, keys, values):
    q_flat, k_flat, v_flat = (
        lax.all_to_all(queries, "uly", split_axis=1, concat_axis=0, tiled=True),
        lax.all_to_all(keys, "uly", split_axis=1, concat_axis=0, tiled=True),
        lax.all_to_all(values, "uly", split_axis=1, concat_axis=0, tiled=True),
    )
    row_count = q_flat.shape[0]
    head_count = q_flat.shape[1] // HEAD_DIM
    q_local = q_flat.reshape(row_count, head_count, HEAD_DIM)
    k_local = k_flat.reshape(row_count, head_count, HEAD_DIM)
    v_local = v_flat.reshape(row_count, head_count, HEAD_DIM)
    scale = HEAD_DIM ** (-0.5)
    row_best, row_total, running = cycle_plan(q_local, k_local, v_local, scale)
    local_out = (
        (running / row_total[..., None])
        .astype(jnp.bfloat16)
        .reshape(row_count, head_count * HEAD_DIM)
    )
    return lax.all_to_all(local_out, "uly", split_axis=0, concat_axis=1, tiled=True)


def solution(mesh):
    placed = (P(("uly", "blk"), None), P(("uly", "blk"), None), P(("uly", "blk"), None))
    return jax.shard_map(
        shards, mesh=mesh, in_specs=placed, out_specs=P(("uly", "blk"), None), check_vma=False
    )
```

profile of v0, /device:TPU:6, one launch (start us, length us, event | category | flops | bytes accessed | tf_op | source)
XLA Modules:
  0.0 386.1 jit_solution(11031178758126498211)
XLA Ops:
  7.5 12.9 %all_to_all.70 = bf16[32,8,384]{2,0,1:T(8,128)(2,1)S(1)} all-to-all(bf16[32,8,384]{2,0,1:T(8,128)(2,1)S(1)} %bitcast.72), channel_id=1, replica_groups=mesh['uly'=8,'blk'=64] {'uly'}, dimensions={1} | all-to-all | bytes 393216 | tf_op jit(solution)/shard_map/all_to_all | solution.py:77
  21.3 9.5 %all_to_all.71 = bf16[32,8,384]{2,0,1:T(8,128)(2,1)S(1)} all-to-all(bf16[32,8,384]{2,0,1:T(8,128)(2,1)S(1)} %bitcast.73), channel_id=1, replica_groups=mesh['uly'=8,'blk'=64] {'uly'}, dimensions={1} | all-to-all | bytes 393216 | tf_op jit(solution)/shard_map/all_to_all | solution.py:78
  32.3 5.7 %all-to-all-start.1 = ((bf16[32,8,384]{2,0,1:T(8,128)(2,1)}), bf16[32,8,384]{2,0,1:T(8,128)(2,1)S(1)}, u32[]{:S(2)}, u32[]{:S(2)}) async-start(bf16[32,8,384]{2,0,1:T(8,128)(2,1)} %bitcast.49), calls=%async_computation.1 | async-start | bytes 393216 | tf_op jit(solution)/shard_map/all_to_all | solution.py:76
  37.9 6.7 %all-to-all-done.1 = bf16[32,8,384]{2,0,1:T(8,128)(2,1)S(1)} async-done(((bf16[32,8,384]{2,0,1:T(8,128)(2,1)}), bf16[32,8,384]{2,0,1:T(8,128)(2,1)S(1)}, u32[]{:S(2)}, u32[]{:S(2)}) %all-to-all-start.1) | async-done | bytes 196640 | tf_op jit(solution)/shard_map/all_to_all | solution.py:76
  44.7 100.4 %all-gather.3.cloned.1.call-done = bf16[16384,3,128]{2,0,1:T(8,128)(2,1)} async-done(((bf16[256,3,128]{2,0,1:T(8,128)(2,1)}), bf16[16384,3,128]{2,0,1:T(8,128)(2,1)}) %all-gather.3.cloned.1.call-update) | async-done | bytes 12582928 | tf_op jit(solution)/shard_map/all_gather | solution.py:59
  145.1 122.0 %all-gather.5.cloned.1.call-done = bf16[16384,3,128]{2,0,1:T(8,128)(2,1)} async-done(((bf16[256,3,128]{2,0,1:T(8,128)(2,1)}), bf16[16384,3,128]{2,0,1:T(8,128)(2,1)}) %all-gather.5.cloned.1.call-update) | async-done | bytes 12582928 | tf_op jit(solution)/shard_map/all_gather | solution.py:60
  267.1 101.4 %while.15 = (s32[]{:T(128)}, f32[256,3]{0,1:T(4,128)S(1)}, f32[256,3]{0,1:T(4,128)S(1)}, f32[256,3,128]{0,2,1:T(8,128)S(1)}, bf16[32,512,3,128]{3,1,0,2:T(8,128)...) while((s32[]{:T(128)}, f32[256,3]{0,1:T(4,128)S(1)}, ...), condition=%wide.region_3.0_spmd.clone, body=%wide.region_0.3_spmd.clone.sunk | while | flops 204083712 | bytes 6532200 | solution.py:70
  268.7 1.5 fusion.26
  270.2 1.4 bitcast_reduce_fusion.2
  271.9 1.5 fusion.26
  273.4 1.4 bitcast_reduce_fusion.2
  275.0 1.5 fusion.26
  276.6 1.4 bitcast_reduce_fusion.2
  278.2 1.5 fusion.26
  279.7 1.4 bitcast_reduce_fusion.2
  281.4 1.5 fusion.26
  284.5 1.5 fusion.26
  286.1 1.4 bitcast_reduce_fusion.2
  287.7 1.5 fusion.26
  289.2 1.4 bitcast_reduce_fusion.2
  290.9 1.5 fusion.26
  292.4 1.4 bitcast_reduce_fusion.2
  294.0 1.5 fusion.26
  295.6 1.4 bitcast_reduce_fusion.2
  297.2 1.5 fusion.26
  300.4 1.5 fusion.26
  301.9 1.4 bitcast_reduce_fusion.2
  303.5 1.5 fusion.26
  305.1 1.4 bitcast_reduce_fusion.2
  306.7 1.5 fusion.26
  308.3 1.4 bitcast_reduce_fusion.2
  309.9 1.5 fusion.26
  311.4 1.4 bitcast_reduce_fusion.2
  313.0 1.5 fusion.26
  316.2 1.5 fusion.26
  317.8 1.4 bitcast_reduce_fusion.2
  319.4 1.5 fusion.26
  320.9 1.4 bitcast_reduce_fusion.2
  322.6 1.5 fusion.26
  324.1 1.4 bitcast_reduce_fusion.2
  325.7 1.5 fusion.26
  327.3 1.4 bitcast_reduce_fusion.2
  328.9 1.5 fusion.26
  332.1 1.5 fusion.26
  333.6 1.4 bitcast_reduce_fusion.2
  335.2 1.5 fusion.26
  336.8 1.4 bitcast_reduce_fusion.2
  338.4 1.5 fusion.26
  339.9 1.4 bitcast_reduce_fusion.2
  341.6 1.5 fusion.26
  343.1 1.4 bitcast_reduce_fusion.2
  344.7 1.5 fusion.26
  347.9 1.5 fusion.26
  349.4 1.4 bitcast_reduce_fusion.2
  351.1 1.5 fusion.26
  352.6 1.4 bitcast_reduce_fusion.2
  354.2 1.5 fusion.26
  355.8 1.4 bitcast_reduce_fusion.2
  357.4 1.5 fusion.26
  360.6 1.5 fusion.26
  363.7 1.5 fusion.26
  365.3 1.4 bitcast_reduce_fusion.2
  366.9 1.5 fusion.26
  368.8 9.7 %all_to_all.72 = bf16[8,32,384]{2,1,0:T(8,128)(2,1)S(1)} all-to-all(bf16[8,32,384]{2,1,0:T(8,128)(2,1)S(1)} %all_to_all.62), channel_id=1, replica_groups=mesh['uly'=8,'blk'=64] {'uly'}, dimensions={0} | all-to-all | bytes 393216 | tf_op jit(solution)/shard_map/all_to_all | solution.py:92
  (95 shorter events, 23.6 us)
Async XLA Ops:
  6.5 14.7 %copy-start = (bf16[32,3072]{1,0:T(8,128)(2,1)S(1)}, bf16[32,3072]{1,0:T(8,128)(2,1)}, u32[]{:S(2)}) copy-start(bf16[32,3072]{1,0:T(8,128)(2,1)} %param.7) | copy-start | bytes 589828
  6.5 138.5 %all-gather.3.cloned.1.call-start = ((), (), s32[]{:S(2)}) async-start(), calls=%async_computation.4 | async-start | bytes 12779520 | tf_op jit(solution)/shard_map/all_gather | solution.py:59
  20.4 11.2 %copy-start.1 = (bf16[32,3072]{1,0:T(8,128)(2,1)S(1)}, bf16[32,3072]{1,0:T(8,128)(2,1)}, u32[]{:S(2)}) copy-start(bf16[32,3072]{1,0:T(8,128)(2,1)} %param.5) | copy-start | bytes 589828
  21.2 245.9 %all-gather.5.cloned.1.call-start = ((), (), s32[]{:S(2)}) async-start(), calls=%async_computation.5 | async-start | bytes 12779520 | tf_op jit(solution)/shard_map/all_gather | solution.py:60
  32.3 12.3 %all-to-all-start.1 = ((bf16[32,8,384]{2,0,1:T(8,128)(2,1)}), bf16[32,8,384]{2,0,1:T(8,128)(2,1)S(1)}, u32[]{:S(2)}, u32[]{:S(2)}) async-start(bf16[32,8,384]{2,0,1:T(8,128)(2,1)} %bitcast.49), calls=%async_computation.1 | async-start | bytes 393216 | tf_op jit(solution)/shard_map/all_to_all | solution.py:76
Sparse Core Ops, SparseCore 0:
  21.3 123.7 all-gather.2
  148.4 118.5 all-gather.4
where the time goes:
time: 391 us; the launch traced here: 386 us
  waiting for transfers between devices  229 us (59%)
  matrix products  92.2 us (24%)
  blocking collectives  32.1 us (8%)
  between operations  13.5 us (3%)
  other arithmetic  8.14 us (2%)
  starting transfers between devices  5.7 us (1%)
  local copies, waits for them, and re-layouts  4.44 us (1%)
    all_gather x1, waiting for transfers between devices, cycle_plan(): value_piece = lax.all_gather(v_local, 'blk', axis=0, tiled=True)  122 us
    all_gather x1, waiting for transfers between devices, cycle_plan(): key_piece = lax.all_gather(k_local, 'blk', axis=0, tiled=True)  100 us
    dot_general x32, matrix products, one_block(): jnp.einsum('qhk,khd->qhd', expo_vals.astype(jnp.bfloat16), value_rows, pr...  48.6 us
    dot_general x32, matrix products, one_block(): jnp.einsum('qhd,khd->qhk', q_block, key_rows, preferred_element_type=jnp....  43.6 us
    all_to_all x1, blocking collectives, shards(): lax.all_to_all(keys, 'uly', split_axis=1, concat_axis=0, tiled=True)  12.9 us
    all_to_all x1, blocking collectives, shards(): lax.all_to_all(local_out, 'uly', split_axis=0, concat_axis=1, tiled=True)  9.73 us
    all_to_all x1, blocking collectives, shards(): lax.all_to_all(values, 'uly', split_axis=1, concat_axis=0, tiled=True)  9.46 us
  transfers between devices with their start and end apart: 3, of which 3 were waited for; matrix products, arithmetic and copies ran while one was open for 0% of the time, Pallas kernels for 0%

commit v1 on v0

v1 whole, which is shorter than its diff:
```python
import functools
import math

import jax
import jax.numpy as jnp
from jax import lax
from jax.experimental import pallas as pl
from jax.experimental.pallas import tpu as pltpu
from jax.sharding import Mesh, PartitionSpec as P

HEAD_DIM = 128
STAT_ROWS = 16
EXPONENT = HEAD_DIM**-0.5 * math.log2(math.e)


def attend_kernel(q_ref, kv_ref, out_ref):
    rows = q_ref.shape[0]
    heads = q_ref.shape[1] // HEAD_DIM
    keys_n = kv_ref.shape[0] * kv_ref.shape[2]
    shifts, totals = [], []
    for h in range(heads):
        cols = slice(h * HEAD_DIM, (h + 1) * HEAD_DIM)
        k = kv_ref[:, 0, :, cols].reshape(keys_n, HEAD_DIM)
        v = kv_ref[:, 1, :, cols].reshape(keys_n, HEAD_DIM)
        s = lax.dot_general(
            q_ref[:, cols], k, (((1,), (1,)), ((), ())), preferred_element_type=jnp.float32
        )
        top = jnp.max(s, axis=1, keepdims=True) * EXPONENT
        shift = top.astype(jnp.bfloat16).astype(jnp.float32)
        e = jnp.exp2(s * EXPONENT - shift)
        total = jnp.sum(e, axis=1, keepdims=True)
        o = jnp.dot(e.astype(jnp.bfloat16), v, preferred_element_type=jnp.float32)
        out_ref[0, 0:rows, cols] = o.astype(jnp.bfloat16)
        shifts.append(shift)
        totals.append(total)
    lane = lax.broadcasted_iota(jnp.int32, (rows, HEAD_DIM), 1)
    stats = jnp.zeros((rows, HEAD_DIM), jnp.float32)
    for h in range(heads):
        high = totals[h].astype(jnp.bfloat16).astype(jnp.float32)
        stats = jnp.where(lane == h, shifts[h], stats)
        stats = jnp.where(lane == heads + h, high, stats)
        stats = jnp.where(lane == 2 * heads + h, totals[h] - high, stats)
    out_ref[0, rows : rows + STAT_ROWS, 0:rows] = stats.T[0:STAT_ROWS].astype(jnp.bfloat16)
    out_ref[0, rows : rows + STAT_ROWS, rows:] = jnp.zeros(
        (STAT_ROWS, out_ref.shape[2] - rows), jnp.bfloat16
    )


def attend(q, kv):
    pieces, _, piece_rows, width = kv.shape
    rows = piece_rows
    blocks = q.shape[0] // rows
    heads = width // HEAD_DIM
    keys_n = pieces * piece_rows
    return pl.pallas_call(
        attend_kernel,
        grid=(blocks,),
        in_specs=[
            pl.BlockSpec((rows, width), lambda i: (i, 0)),
            pl.BlockSpec((pieces, 2, piece_rows, width), lambda i: (0, 0, 0, 0)),
        ],
        out_specs=pl.BlockSpec((1, rows + STAT_ROWS, width), lambda i: (i, 0, 0)),
        out_shape=jax.ShapeDtypeStruct((blocks, rows + STAT_ROWS, width), jnp.bfloat16),
        compiler_params=pltpu.CompilerParams(vmem_limit_bytes=48 * 2**20),
        cost_estimate=pl.CostEstimate(
            flops=4 * q.shape[0] * keys_n * width,
            bytes_accessed=2 * (2 * q.size + kv.size),
            transcendentals=q.shape[0] * keys_n * heads,
        ),
    )(q, kv)


def merge_kernel(parts_ref, out_ref):
    pieces = parts_ref.shape[0]
    rows, width = out_ref.shape
    heads = width // HEAD_DIM
    stats = [
        parts_ref[p, rows : rows + STAT_ROWS, 0:rows].astype(jnp.float32) for p in range(pieces)
    ]
    shifts = [s[0:heads] for s in stats]
    totals = [s[heads : 2 * heads] + s[2 * heads : 3 * heads] for s in stats]
    best = functools.reduce(jnp.maximum, shifts)
    factors = [jnp.exp2(s - best) for s in shifts]
    denom = sum(f * t for f, t in zip(factors, totals))
    weights = jnp.concatenate([f / denom for f in factors], axis=0)
    pad = jnp.zeros((HEAD_DIM - weights.shape[0], rows), jnp.float32)
    weights = jnp.concatenate([weights, pad], axis=0).T
    for h in range(heads):
        cols = slice(h * HEAD_DIM, (h + 1) * HEAD_DIM)
        total = jnp.zeros((rows, HEAD_DIM), jnp.float32)
        for p in range(pieces):
            w = weights[:, p * heads + h : p * heads + h + 1]
            total = total + w * parts_ref[p, 0:rows, cols].astype(jnp.float32)
        out_ref[:, cols] = total.astype(jnp.bfloat16)


def merge(parts):
    pieces, part_rows, width = parts.shape
    return pl.pallas_call(
        merge_kernel,
        out_shape=jax.ShapeDtypeStruct((part_rows - STAT_ROWS, width), jnp.bfloat16),
        in_specs=[pl.BlockSpec(memory_space=pltpu.VMEM)],
        out_specs=pl.BlockSpec(memory_space=pltpu.VMEM),
        compiler_params=pltpu.CompilerParams(vmem_limit_bytes=32 * 2**20),
    )(parts)


HEAD_AXES = ("x", "zl")
KEY_AXES = ("y",)
ROW_AXES = ("zh", "c")
ALL_AXES = ("x", "zl", "y", "zh", "c")


def shards(queries, keys, values):
    rows = queries.shape[0]
    groups = 8
    width = queries.shape[1] // groups
    stacked = jnp.stack([a.reshape(rows, groups, width) for a in (keys, values, queries)])
    stacked = stacked.transpose(2, 0, 1, 3)
    mine = lax.all_to_all(stacked, HEAD_AXES, split_axis=0, concat_axis=0, tiled=True)
    mine = mine.transpose(1, 0, 2, 3).reshape(3, groups * rows, width)
    kv = lax.all_gather(mine[0:2], KEY_AXES, axis=0, tiled=False)
    q = lax.all_gather(mine[2], ROW_AXES, axis=0, tiled=True)
    parts = attend(q, kv)
    parts = lax.all_to_all(parts, ROW_AXES, split_axis=0, concat_axis=0, tiled=True)
    merged = merge(parts).reshape(groups, rows, width)
    spread = lax.all_to_all(merged, HEAD_AXES, split_axis=0, concat_axis=0, tiled=True)
    return spread.transpose(1, 0, 2).reshape(rows, groups * width)


def solution(mesh):
    fine = Mesh(mesh.devices.reshape(4, 2, 8, 4, 2), ALL_AXES)
    placed = P(ALL_AXES, None)
    return jax.shard_map(
        shards, mesh=fine, in_specs=(placed,) * 3, out_specs=placed, check_vma=False
    )
```

time: 391 us -> 208 us (0.53)
  waiting for transfers between devices: 229 us -> 86.6 us
  matrix products: 92.2 us -> 0 us
  blocking collectives: 32.1 us -> 74.7 us
  Pallas kernels: 0 us -> 24.9 us
  other arithmetic: 8.14 us -> 0.08 us
  starting transfers between devices: 5.7 us -> 0.04 us
    all_gather x2, waiting for transfers between devices: 222 us -> 86.6 us  [the longest x1 47.8 us: shards(): kv = lax.all_gather(mine[0:2], KEY_AXES, axis=0, tiled=False)]
    dot_general x64 -> x0, matrix products: 92.2 us -> none  [the longest x32 48.6 us: one_block(): jnp.einsum('qhk,khd->qhd', expo_vals.astype(jnp.bfloat16), value_rows, pr...]
    all_to_all x3, blocking collectives: 32.1 us -> 74.7 us  [the longest x1 49.7 us: shards(): lax.all_to_all(parts, ROW_AXES, split_axis=0, concat_axis=0, tiled=True)]
    pallas_call x0 -> x2, Pallas kernels: none -> 24.9 us  [the longest x1 23.9 us: attend(): pl.pallas_call(attend_kernel, grid=(blocks,), in_specs=[pl.BlockSpec((row...]
    reduce_sum x32 -> x0, other arithmetic: 7.33 us -> none  [one_block(): total = jnp.sum(expo_vals, axis=2)]
    all_to_all x1 -> x0, waiting for transfers between devices: 6.65 us -> none  [shards(): lax.all_to_all(queries, 'uly', split_axis=1, concat_axis=0, tiled=True)]
    all_to_all x1 -> x0, starting transfers between devices: 5.66 us -> none  [shards(): lax.all_to_all(queries, 'uly', split_axis=1, concat_axis=0, tiled=True)]
    unnamed x5, local copies, waits for them, and re-layouts: 0.15 us -> 4.26 us
  transfers between devices with their start and end apart: 3 -> 2, of which waited for: 3 -> 2; matrix products, arithmetic and copies ran while one was open for 0% -> 0% of each run, Pallas kernels for 0% -> 0%
where the time goes in v1:
time: 208 us; the launch traced here: 206 us
  waiting for transfers between devices  86.6 us (42%)
  blocking collectives  74.7 us (36%)
  Pallas kernels  24.9 us (12%)
  between operations  13.4 us (6%)
  local copies, waits for them, and re-layouts  6.63 us (3%)
    all_to_all x1, blocking collectives, shards(): lax.all_to_all(parts, ROW_AXES, split_axis=0, concat_axis=0, tiled=True)  49.7 us
    all_gather x1, waiting for transfers between devices, shards(): kv = lax.all_gather(mine[0:2], KEY_AXES, axis=0, tiled=False)  47.8 us
    all_gather x1, waiting for transfers between devices, shards(): q = lax.all_gather(mine[2], ROW_AXES, axis=0, tiled=True)  38.8 us
    pallas_call x1, Pallas kernels, attend(): pl.pallas_call(attend_kernel, grid=(blocks,), in_specs=[pl.BlockSpec((row...  23.9 us
    all_to_all x1, blocking collectives, shards(): lax.all_to_all(stacked, HEAD_AXES, split_axis=0, concat_axis=0, tiled=True)  15.3 us
    all_to_all x1, blocking collectives, shards(): lax.all_to_all(merged, HEAD_AXES, split_axis=0, concat_axis=0, tiled=True)  9.74 us
    unnamed x5, local copies, waits for them, and re-layouts  4.26 us
  transfers between devices with their start and end apart: 2, of which 2 were waited for; matrix products, arithmetic and copies ran while one was open for 0% of the time, Pallas kernels for 0%

profile of v1, /device:TPU:6, one launch (start us, length us, event | category | flops | bytes accessed | tf_op | source)
XLA Modules:
  0.0 206.5 jit_solution(5840030218541422464)
XLA Ops:
  6.5 0.0 all-gather.3.cloned.1.call-start
  6.5 0.9 copy.15
  7.5 1.0 copy.13
  8.4 1.0 copy.14
  9.4 0.1 maximum_bitcast_fusion
  9.5 0.1 copy.9
  9.6 15.3 %all_to_all.15 = bf16[8,3,32,384]{3,2,1,0:T(8,128)(2,1)S(1)} all-to-all(bf16[8,3,32,384]{3,2,1,0:T(8,128)(2,1)S(1)} %copy.9), channel_id=1, replica_groups=mesh['x'=4,'zl'=2,'y'=8,'zh'=4,'c'=2] {'x','zl'}, dimensions={0} | all-to-all | bytes 1179648 | tf_op jit(solution)/shard_map/all_to_all | solution.py:120
  24.9 0.1 copy.17
  25.0 0.7 slice.10
  25.7 0.0 all-gather.3.cloned.1.call-update
  25.7 0.0 all-gather.5.cloned.1.call-start
  25.7 0.8 slice.11
  26.6 0.0 all-gather.5.cloned.1.call-update
  26.6 38.8 %all-gather.3.cloned.1.call-done.q_ref = bf16[2048,384]{1,0:T(8,128)(2,1)} async-done(((bf16[256,384]{1,0:T(8,128)(2,1)}), bf16[2048,384]{1,0:T(8,128)(2,1)}) %all-gather.3.cloned.1.call-update) | async-done | bytes 1572880 | tf_op jit(solution)/shard_map/all_gather | solution.py:123
  65.4 47.8 %all-gather.5.cloned.1.call-done.kv_ref = bf16[8,2,256,384]{3,2,1,0:T(8,128)(2,1)} async-done(((bf16[1,2,256,384]{3,2,1,0:T(8,128)(2,1)}), bf16[8,2,256,384]{3,2,1,0:T(8,128)(2,1)}) %all-gather.5.cloned.1.call-update) | async-done | bytes 3145744 | tf_op jit(solution)/shard_map/all_gather | solution.py:122
  113.2 0.0 copy-start
  113.2 1.4 copy-done
  114.6 23.9 %shard_map.37 = bf16[8,272,384]{2,1,0:T(8,128)(2,1)S(1)} custom-call(bf16[2048,384]{1,0:T(8,128)(2,1)S(1)} %copy-done, bf16[8,2,256,384]{3,2,1,0:T(8,128)(2,1)} %all-gather.5.cloned.1.call-done.kv_ref), custom_call_target="tpu_custom_call" | custom-call | flops 6442450944 | bytes 6291456 | tf_op jit(solution)/shard_map/pallas_call | solution.py:55
  138.4 49.7 %all_to_all.16.parts_ref = bf16[8,272,384]{2,1,0:T(8,128)(2,1)S(1)} all-to-all(bf16[8,272,384]{2,1,0:T(8,128)(2,1)S(1)} %shard_map.37), channel_id=1, replica_groups=mesh['x'=4,'zl'=2,'y'=8,'zh'=4,'c'=2] {'zh','c'}, dimensions={0} | all-to-all | bytes 3342336 | tf_op jit(solution)/shard_map/all_to_all | solution.py:125
  188.1 1.1 shard_map.38
  189.2 9.7 %all_to_all.17 = bf16[8,32,384]{2,1,0:T(8,128)(2,1)S(1)} all-to-all(bf16[8,32,384]{2,1,0:T(8,128)(2,1)S(1)} %bitcast.20), channel_id=1, replica_groups=mesh['x'=4,'zl'=2,'y'=8,'zh'=4,'c'=2] {'x','zl'}, dimensions={0} | all-to-all | bytes 393216 | tf_op jit(solution)/shard_map/all_to_all | solution.py:127
  198.9 0.7 copy.12
Async XLA Ops:
  6.5 58.9 %all-gather.3.cloned.1.call-start = ((), (), s32[]{:S(2)}) async-start(), calls=%async_computation.3 | async-start | bytes 1769472 | tf_op jit(solution)/shard_map/all_gather | solution.py:123
  25.7 87.5 %all-gather.5.cloned.1.call-start = ((), (), s32[]{:S(2)}) async-start(), calls=%async_computation.4 | async-start | bytes 3538944 | tf_op jit(solution)/shard_map/all_gather | solution.py:122
  113.2 1.4 copy-start
Sparse Core Ops, SparseCore 0:
  25.8 39.5 all-gather.2
  67.5 45.6 all-gather.4

commit v2 on v1

v2 whole, which is shorter than its diff:
```python
import functools
import math

import jax
import jax.numpy as jnp
from jax import lax
from jax.experimental import pallas as pl
from jax.experimental.pallas import tpu as pltpu
from jax.sharding import Mesh, PartitionSpec as P

HEAD_DIM = 128
STAT_ROWS = 16
KEY_CHUNK = 512
EXPONENT = HEAD_DIM**-0.5 * math.log2(math.e)


def head_cols(h):
    return slice(h * HEAD_DIM, (h + 1) * HEAD_DIM)


def attend_kernel(at_ref, q_ref, kv_ref, *refs):
    out_refs, score_refs = refs[:-2], refs[-2:]
    out_rows, width = out_refs[0].shape
    rows = out_rows - STAT_ROWS
    heads = width // HEAD_DIM
    unit_rows = score_refs[0].shape[0]
    slabs, runs, _, run, _ = kv_ref.shape
    keys_n = slabs * runs * run
    chunks = keys_n // KEY_CHUNK
    slab_step = slabs // chunks

    def kv_chunk(which, h, j):
        block = kv_ref[j * slab_step : (j + 1) * slab_step, :, which, :, head_cols(h)]
        return block.reshape(KEY_CHUNK, HEAD_DIM)

    def score_chunk(q, h, j, top):
        s = lax.dot_general(
            q, kv_chunk(0, h, j), (((1,), (1,)), ((), ())), preferred_element_type=jnp.float32
        )
        score_refs[h % 2][:, j * KEY_CHUNK : (j + 1) * KEY_CHUNK] = s
        for t in range(KEY_CHUNK // HEAD_DIM):
            part = s[:, head_cols(t)]
            top = part if top is None else jnp.maximum(top, part)
        return top

    def query(h):
        return jnp.concatenate(
            [q_ref[at_ref[b], :, head_cols(h)] for b in range(len(out_refs))], axis=0
        )

    def shift_of(top):
        best = jnp.max(top, axis=1, keepdims=True) * EXPONENT
        return best.astype(jnp.bfloat16).astype(jnp.float32)

    ones = jnp.ones((KEY_CHUNK, HEAD_DIM), jnp.bfloat16)
    top = None
    q = query(0)
    for j in range(chunks):
        top = score_chunk(q, 0, j, top)
    shift = shift_of(top)
    lane = lax.broadcasted_iota(jnp.int32, (unit_rows, HEAD_DIM), 1)
    stats = jnp.zeros((unit_rows, HEAD_DIM), jnp.float32)
    for h in range(heads):
        more = h + 1 < heads
        top, total = None, None
        if more:
            q = query(h + 1)
        for j in range(chunks):
            if more:
                top = score_chunk(q, h + 1, j, top)
            s = score_refs[h % 2][:, j * KEY_CHUNK : (j + 1) * KEY_CHUNK]
            e = jnp.exp2(s * EXPONENT - shift).astype(jnp.bfloat16)
            v = jnp.concatenate([kv_chunk(1, h, j), ones], axis=1)
            o = jnp.dot(e, v, preferred_element_type=jnp.float32)
            total = o if total is None else total + o
        for b, out_ref in enumerate(out_refs):
            part = total[b * rows : (b + 1) * rows, 0:HEAD_DIM]
            out_ref[0:rows, head_cols(h)] = part.astype(jnp.bfloat16)
        denom = total[:, HEAD_DIM:]
        high = denom.astype(jnp.bfloat16).astype(jnp.float32)
        stats = jnp.where(lane == h, shift, stats)
        stats = jnp.where(lane == heads + h, high, stats)
        stats = jnp.where(lane == 2 * heads + h, denom - high, stats)
        if more:
            shift = shift_of(top)
    flipped = stats.T[0:STAT_ROWS].astype(jnp.bfloat16)
    for b, out_ref in enumerate(out_refs):
        out_ref[rows:, 0:rows] = flipped[:, b * rows : (b + 1) * rows]
        out_ref[rows:, rows:] = jnp.zeros((STAT_ROWS, width - rows), jnp.bfloat16)


def attend(at, q, kv):
    count = at.shape[0]
    _, rows, width = q.shape
    heads = width // HEAD_DIM
    keys_n = kv.size // (2 * width)
    vmem = pl.BlockSpec(memory_space=pltpu.VMEM)
    return pl.pallas_call(
        attend_kernel,
        in_specs=[pl.BlockSpec(memory_space=pltpu.SMEM), vmem, vmem],
        out_specs=[vmem] * count,
        out_shape=[jax.ShapeDtypeStruct((rows + STAT_ROWS, width), jnp.bfloat16)] * count,
        scratch_shapes=[pltpu.VMEM((count * rows, keys_n), jnp.float32)] * 2,
        compiler_params=pltpu.CompilerParams(vmem_limit_bytes=28 * 2**20),
        cost_estimate=pl.CostEstimate(
            flops=4 * count * rows * keys_n * width,
            bytes_accessed=2 * (2 * count * rows * width + kv.size),
            transcendentals=count * rows * keys_n * heads,
        ),
    )(at, q, kv)


def merge_kernel(*refs):
    *part_refs, out_ref = refs
    rows, width = out_ref.shape
    heads = width // HEAD_DIM
    stats = [
        ref[rows : rows + STAT_ROWS, 0:rows].astype(jnp.float32) for ref in part_refs
    ]
    shifts = [s[0:heads] for s in stats]
    totals = [s[heads : 2 * heads] + s[2 * heads : 3 * heads] for s in stats]
    best = functools.reduce(jnp.maximum, shifts)
    factors = [jnp.exp2(s - best) for s in shifts]
    denom = sum(f * t for f, t in zip(factors, totals))
    weights = jnp.concatenate([f / denom for f in factors], axis=0)
    pad = jnp.zeros((HEAD_DIM - weights.shape[0], rows), jnp.float32)
    weights = jnp.concatenate([weights, pad], axis=0).T
    for h in range(heads):
        total = jnp.zeros((rows, HEAD_DIM), jnp.float32)
        for p, ref in enumerate(part_refs):
            w = weights[:, p * heads + h : p * heads + h + 1]
            total = total + w * ref[0:rows, head_cols(h)].astype(jnp.float32)
        out_ref[:, head_cols(h)] = total.astype(jnp.bfloat16)


def merge(parts):
    part_rows, width = parts[0].shape
    return pl.pallas_call(
        merge_kernel,
        out_shape=jax.ShapeDtypeStruct((part_rows - STAT_ROWS, width), jnp.bfloat16),
        in_specs=[pl.BlockSpec(memory_space=pltpu.VMEM)] * len(parts),
        out_specs=pl.BlockSpec(memory_space=pltpu.VMEM),
        compiler_params=pltpu.CompilerParams(vmem_limit_bytes=32 * 2**20),
    )(*parts)


def split_kernel(*refs):
    *in_refs, out_ref = refs
    groups, arrays, rows, width = out_ref.shape
    for g in range(groups):
        for a in range(arrays):
            out_ref[g, a] = in_refs[a][:, g * width : (g + 1) * width]


def split(groups, *arrays):
    rows, columns = arrays[0].shape
    return pl.pallas_call(
        split_kernel,
        out_shape=jax.ShapeDtypeStruct(
            (groups, len(arrays), rows, columns // groups), arrays[0].dtype
        ),
        in_specs=[pl.BlockSpec(memory_space=pltpu.VMEM)] * len(arrays),
        out_specs=pl.BlockSpec(memory_space=pltpu.VMEM),
    )(*arrays)


HEAD_AXES = ("zh", "zl")
KEY_AXES = ("y",)
ROW_AXES = ("x", "c")
ALL_AXES = ("x", "zl", "y", "zh", "c")


def exchange(array, axes):
    return lax.all_to_all(array, axes, split_axis=0, concat_axis=0, tiled=True)


def attend_and_send(q, kv, step):
    chips, cores = lax.axis_size("x"), lax.axis_size("c")
    chip = lax.rem(lax.axis_index("x") + step, chips)
    core = lax.axis_index("c")
    at = jnp.stack([chip * cores + core, chip * cores + (1 - core)]).astype(jnp.int32)
    parts = attend(at, q, kv)
    arrived = []
    for other, part in enumerate(parts):
        if step or other:
            perm = [
                (x * cores + c, (x + step) % chips * cores + (c + other) % cores)
                for x in range(chips)
                for c in range(cores)
            ]
            part = lax.ppermute(part, ROW_AXES, perm)
        arrived.append(part)
    return arrived


def shards(queries, keys, values):
    groups = lax.axis_size(HEAD_AXES)
    blocks = lax.axis_size(ROW_AXES)
    rows, columns = queries.shape
    width = columns // groups
    kv = exchange(split(groups, keys, values), HEAD_AXES)
    kv = lax.all_gather(kv, KEY_AXES, axis=0, tiled=False)
    q = exchange(split(groups, queries), HEAD_AXES).reshape(1, groups * rows, width)
    q = exchange(jnp.broadcast_to(q, (blocks, groups * rows, width)), ROW_AXES)
    parts = []
    for step in (2, 1, 3, 0):
        parts += attend_and_send(q, kv, step)
    merged = merge(parts).reshape(groups, rows, width)
    spread = exchange(merged, HEAD_AXES)
    return spread.transpose(1, 0, 2).reshape(rows, columns)


def solution(mesh):
    fine = Mesh(mesh.devices.reshape(4, 2, 8, 4, 2), ALL_AXES)
    placed = P(ALL_AXES, None)
    return jax.shard_map(
        shards, mesh=fine, in_specs=(placed,) * 3, out_specs=placed, check_vma=False
    )
```

time: 208 us -> 149 us (0.72)
  waiting for transfers between devices: 86.6 us -> 27.8 us
  starting transfers between devices: 0.04 us -> 25.4 us
  blocking collectives: 74.7 us -> 56 us
  Pallas kernels: 24.9 us -> 21.6 us
  local copies, waits for them, and re-layouts: 6.63 us -> 3.88 us
    all_gather x2 -> x1, waiting for transfers between devices: 86.6 us -> 3.43 us  [shards(): kv = lax.all_gather(kv, KEY_AXES, axis=0, tiled=False)]
    ppermute x0 -> x7, starting transfers between devices: none -> 20.7 us  [attend_and_send(): part = lax.ppermute(part, ROW_AXES, perm)]
    all_to_all x0 -> x1, waiting for transfers between devices: none -> 19.2 us  [exchange(): return lax.all_to_all(array, axes, split_axis=0, concat_axis=0, tiled=True)]
    all_to_all x3, blocking collectives: 74.7 us -> 56 us  [exchange(): return lax.all_to_all(array, axes, split_axis=0, concat_axis=0, tiled=True)]
    ppermute x0 -> x7, waiting for transfers between devices: none -> 5.15 us  [attend_and_send(): part = lax.ppermute(part, ROW_AXES, perm)]
    all_to_all x0 -> x1, starting transfers between devices: none -> 4.78 us  [exchange(): return lax.all_to_all(array, axes, split_axis=0, concat_axis=0, tiled=True)]
    pallas_call x1 -> x6, Pallas kernels: 23.9 us -> 20.5 us  [the longest x4 17.1 us: attend(): pl.pallas_call(attend_kernel, in_specs=[pl.BlockSpec(memory_space=pltpu.S...]
    unnamed x5 -> x2, local copies, waits for them, and re-layouts: 4.26 us -> 1.89 us
  transfers between devices with their start and end apart: 2 -> 9, of which waited for: 2 -> 3; matrix products, arithmetic and copies ran while one was open for 0% -> 1% of each run, Pallas kernels for 0% -> 10%
where the time goes in v2:
time: 149 us
  blocking collectives  56 us (38%)
  waiting for transfers between devices  27.8 us (19%)
  starting transfers between devices  25.4 us (17%)
  Pallas kernels  21.6 us (14%)
  between operations  13.5 us (9%)
  local copies, waits for them, and re-layouts  3.88 us (3%)
    all_to_all x3, blocking collectives, exchange(): return lax.all_to_all(array, axes, split_axis=0, concat_axis=0, tiled=True)  56 us
    ppermute x7, starting transfers between devices, attend_and_send(): part = lax.ppermute(part, ROW_AXES, perm)  20.7 us
    all_to_all x1, waiting for transfers between devices, exchange(): return lax.all_to_all(array, axes, split_axis=0, concat_axis=0, tiled=True)  19.2 us
    pallas_call x4, Pallas kernels, attend(): pl.pallas_call(attend_kernel, in_specs=[pl.BlockSpec(memory_space=pltpu.S...  17.1 us
    ppermute x7, waiting for transfers between devices, attend_and_send(): part = lax.ppermute(part, ROW_AXES, perm)  5.15 us
    all_to_all x1, starting transfers between devices, exchange(): return lax.all_to_all(array, axes, split_axis=0, concat_axis=0, tiled=True)  4.78 us
    pallas_call x2, Pallas kernels, split(): pl.pallas_call(split_kernel, out_shape=jax.ShapeDtypeStruct((groups, len(...  3.44 us
    all_gather x1, waiting for transfers between devices, shards(): kv = lax.all_gather(kv, KEY_AXES, axis=0, tiled=False)  3.43 us
  transfers between devices with their start and end apart: 9, of which 3 were waited for; matrix products, arithmetic and copies ran while one was open for 1% of the time, Pallas kernels for 10%

profile of v2, /device:TPU:6, one launch (start us, length us, event | category | flops | bytes accessed | tf_op | source)
XLA Modules:
  0.0 148.5 jit_solution(10108982765691817581)
XLA Ops:
  6.5 0.0 all-gather.3.cloned.1.call-start
  6.5 1.8 %shard_map.38 = bf16[8,2,32,384]{3,2,1,0:T(8,128)(2,1)} custom-call(bf16[32,3072]{1,0:T(8,128)(2,1)} %refs_0_.3, bf16[32,3072]{1,0:T(8,128)(2,1)} %refs_1_.1), custom_call_target="tpu_custom_call" | custom-call | tf_op jit(solution)/shard_map/pallas_call | solution.py:157
  8.4 25.1 %all_to_all.20 = bf16[8,2,32,384]{3,2,1,0:T(8,128)(2,1)} all-to-all(bf16[8,2,32,384]{3,2,1,0:T(8,128)(2,1)} %shard_map.38), channel_id=1, replica_groups=mesh['x'=4,'zl'=2,'y'=8,'zh'=4,'c'=2] {'zh','zl'}, dimensions={0} | all-to-all | bytes 786432 | tf_op jit(solution)/shard_map/all_to_all | solution.py:174
  33.5 0.0 all-gather.3.cloned.1.call-update
  33.5 1.6 %shard_map.37 = bf16[8,1,32,384]{3,2,1,0:T(8,128)(2,1)} custom-call(bf16[32,3072]{1,0:T(8,128)(2,1)} %refs_0_.2), custom_call_target="tpu_custom_call" | custom-call | tf_op jit(solution)/shard_map/pallas_call | solution.py:157
  35.1 13.1 %all_to_all.21 = bf16[8,1,32,384]{3,2,1,0:T(8,128)(2,1)S(1)} all-to-all(bf16[8,1,32,384]{3,2,1,0:T(8,128)(2,1)} %shard_map.37), channel_id=1, replica_groups=mesh['x'=4,'zl'=2,'y'=8,'zh'=4,'c'=2] {'zh','zl'}, dimensions={0} | all-to-all | bytes 393216 | tf_op jit(solution)/shard_map/all_to_all | solution.py:174
  48.2 1.3 broadcast_in_dim.8
  49.5 4.8 %all-to-all-start.1 = ((bf16[8,256,384]{2,1,0:T(8,128)(2,1)}), bf16[8,256,384]{2,1,0:T(8,128)(2,1)S(1)}, u32[]{:S(2)}, u32[]{:S(2)}) async-start(bf16[8,256,384]{2,1,0:T(8,128)(2,1)} %broadcast_in_dim.8), calls=%async_computation.1 | async-start | bytes 3145728 | tf_op jit(solution)/shard_map/all_to_all | solution.py:174
  54.2 0.1 pad_add_fusion.at_ref
  54.3 0.1 pad_add_fusion.1.at_ref
  54.4 0.1 pad_add_fusion.2.at_ref
  54.5 0.1 pad_add_fusion.3.at_ref
  54.6 19.2 %all-to-all-done.1.q_ref = bf16[8,256,384]{2,1,0:T(8,128)(2,1)S(1)} async-done(((bf16[8,256,384]{2,1,0:T(8,128)(2,1)}), bf16[8,256,384]{2,1,0:T(8,128)(2,1)S(1)}, u32[]{:S(2)}, u32[]{:S(2)}) %all-to-all-start.1) | async-done | bytes 1572896 | tf_op jit(solution)/shard_map/all_to_all | solution.py:174
  73.8 3.4 %all-gather.3.cloned.1.call-done = bf16[64,2,32,384]{3,2,1,0:T(8,128)(2,1)} async-done(((bf16[8,2,32,384]{3,2,1,0:T(8,128)(2,1)}), bf16[64,2,32,384]{3,2,1,0:T(8,128)(2,1)}) %all-gather.3.cloned.1.call-update) | async-done | bytes 3145744 | tf_op jit(solution)/shard_map/all_gather | solution.py:202
  77.2 0.0 copy-start
  77.2 1.9 %copy-done = bf16[64,2,32,384]{3,2,1,0:T(8,128)(2,1)S(1)} copy-done((bf16[64,2,32,384]{3,2,1,0:T(8,128)(2,1)S(1)}, bf16[64,2,32,384]{3,2,1,0:T(8,128)(2,1)}, u32[]{:S(2)}) %copy-start) | copy-done | bytes 3145752
  79.1 4.3 %shard_map.39 = (bf16[272,384]{1,0:T(8,128)(2,1)S(1)}, bf16[272,384]{1,0:T(8,128)(2,1)S(1)}) custom-call(s32[2]{0:T(128)S(1)} %pad_add_fusion.at_ref, bf16[8,256,384]{2,1,0:T(8,128)(2,1)S(1)} %all-to-all-done.1.q_ref, bf16[8,8,2,32,384]{4,3,2,1,0:T(8,128)(2,1)S(1)} %bitcast.15), custom_call_target="tpu_custom_call" | custom-call | flops 1610612736 | bytes 3932160 | tf_op jit(solution)/shard_map/pallas_call | solution.py:98
  83.4 3.4 %collective-permute-start = (bf16[272,384]{1,0:T(8,128)(2,1)S(1)}, bf16[272,384]{1,0:T(8,128)(2,1)S(1)}, u32[]{:S(2)}, u32[]{:S(2)}) collective-permute-start(bf16[272,384]{1,0:T(8,128)(2,1)S(1)} %get-tuple-element.13), channel_id=1, source_target_pairs={{0,256},{1,257},{128,384},{129,385},{256,0},{257,1},{384,128},{385... | collective-permute-start | bytes 626696 | tf_op jit(solution)/shard_map/ppermute | solution.py:191
  86.7 2.6 %collective-permute-start.1 = (bf16[272,384]{1,0:T(8,128)(2,1)S(1)}, bf16[272,384]{1,0:T(8,128)(2,1)S(1)}, u32[]{:S(2)}, u32[]{:S(2)}) collective-permute-start(bf16[272,384]{1,0:T(8,128)(2,1)S(1)} %get-tuple-element.14), channel_id=1, source_target_pairs={{0,257},{1,256},{128,385},{129,384},{256,1},{257,0},{384,129},{385... | collective-permute-start | bytes 626696 | tf_op jit(solution)/shard_map/ppermute | solution.py:191
  89.3 4.3 %shard_map.40 = (bf16[272,384]{1,0:T(8,128)(2,1)S(1)}, bf16[272,384]{1,0:T(8,128)(2,1)S(1)}) custom-call(s32[2]{0:T(128)S(1)} %pad_add_fusion.1.at_ref, bf16[8,256,384]{2,1,0:T(8,128)(2,1)S(1)} %all-to-all-done.1.q_ref, bf16[8,8,2,32,384]{4,3,2,1,0:T(8,128)(2,1)S(1)} %bitcast.16), custom_call_target="tpu_custom_call" | custom-call | flops 1610612736 | bytes 3932160 | tf_op jit(solution)/shard_map/pallas_call | solution.py:98
  93.6 3.3 %collective-permute-start.2 = (bf16[272,384]{1,0:T(8,128)(2,1)S(1)}, bf16[272,384]{1,0:T(8,128)(2,1)S(1)}, u32[]{:S(2)}, u32[]{:S(2)}) collective-permute-start(bf16[272,384]{1,0:T(8,128)(2,1)S(1)} %get-tuple-element.15), channel_id=1, source_target_pairs={{0,128},{1,129},{128,256},{129,257},{256,384},{257,385},{384,0},{3... | collective-permute-start | bytes 626696 | tf_op jit(solution)/shard_map/ppermute | solution.py:191
  96.9 3.5 %collective-permute-start.3 = (bf16[272,384]{1,0:T(8,128)(2,1)S(1)}, bf16[272,384]{1,0:T(8,128)(2,1)S(1)}, u32[]{:S(2)}, u32[]{:S(2)}) collective-permute-start(bf16[272,384]{1,0:T(8,128)(2,1)S(1)} %get-tuple-element.16), channel_id=1, source_target_pairs={{0,129},{1,128},{128,257},{129,256},{256,385},{257,384},{384,1},{3... | collective-permute-start | bytes 626696 | tf_op jit(solution)/shard_map/ppermute | solution.py:191
  100.4 4.3 %shard_map.41 = (bf16[272,384]{1,0:T(8,128)(2,1)S(1)}, bf16[272,384]{1,0:T(8,128)(2,1)S(1)}) custom-call(s32[2]{0:T(128)S(1)} %pad_add_fusion.2.at_ref, bf16[8,256,384]{2,1,0:T(8,128)(2,1)S(1)} %all-to-all-done.1.q_ref, bf16[8,8,2,32,384]{4,3,2,1,0:T(8,128)(2,1)S(1)} %bitcast.17), custom_call_target="tpu_custom_call" | custom-call | flops 1610612736 | bytes 3932160 | tf_op jit(solution)/shard_map/pallas_call | solution.py:98
  104.7 2.5 %collective-permute-start.4 = (bf16[272,384]{1,0:T(8,128)(2,1)S(1)}, bf16[272,384]{1,0:T(8,128)(2,1)S(1)}, u32[]{:S(2)}, u32[]{:S(2)}) collective-permute-start(bf16[272,384]{1,0:T(8,128)(2,1)S(1)} %get-tuple-element.17), channel_id=1, source_target_pairs={{0,384},{1,385},{128,0},{129,1},{256,128},{257,129},{384,256},{385... | collective-permute-start | bytes 626696 | tf_op jit(solution)/shard_map/ppermute | solution.py:191
  107.3 4.3 %shard_map.42 = (bf16[272,384]{1,0:T(8,128)(2,1)S(1)}, bf16[272,384]{1,0:T(8,128)(2,1)S(1)}) custom-call(s32[2]{0:T(128)S(1)} %pad_add_fusion.3.at_ref, bf16[8,256,384]{2,1,0:T(8,128)(2,1)S(1)} %all-to-all-done.1.q_ref, bf16[8,8,2,32,384]{4,3,2,1,0:T(8,128)(2,1)S(1)} %bitcast.18), custom_call_target="tpu_custom_call" | custom-call | flops 1610612736 | bytes 3932160 | tf_op jit(solution)/shard_map/pallas_call | solution.py:98
  111.5 0.0 collective-permute-done.refs_0_
  111.5 1.9 %collective-permute-start.5 = (bf16[272,384]{1,0:T(8,128)(2,1)S(1)}, bf16[272,384]{1,0:T(8,128)(2,1)S(1)}, u32[]{:S(2)}, u32[]{:S(2)}) collective-permute-start(bf16[272,384]{1,0:T(8,128)(2,1)S(1)} %get-tuple-element.18), channel_id=1, source_target_pairs={{0,385},{1,384},{128,1},{129,0},{256,129},{257,128},{384,257},{385... | collective-permute-start | bytes 626696 | tf_op jit(solution)/shard_map/ppermute | solution.py:191
  113.5 0.0 collective-permute-done.1.refs_1_
  113.5 3.4 %collective-permute-start.6 = (bf16[272,384]{1,0:T(8,128)(2,1)S(1)}, bf16[272,384]{1,0:T(8,128)(2,1)S(1)}, u32[]{:S(2)}, u32[]{:S(2)}) collective-permute-start(bf16[272,384]{1,0:T(8,128)(2,1)S(1)} %get-tuple-element.20), channel_id=1, source_target_pairs={{0,1},{1,0},{128,129},{129,128},{256,257},{257,256},{384,385},{385... | collective-permute-start | bytes 626696 | tf_op jit(solution)/shard_map/ppermute | solution.py:191
  116.9 0.0 collective-permute-done.2.refs_2_
  116.9 0.0 collective-permute-done.3.refs_3_
  116.9 0.0 collective-permute-done.4.refs_4_
  116.9 5.1 %collective-permute-done.5.refs_5_ = bf16[272,384]{1,0:T(8,128)(2,1)S(1)} collective-permute-done((bf16[272,384]{1,0:T(8,128)(2,1)S(1)}, bf16[272,384]{1,0:T(8,128)(2,1)S(1)}, u32[]{:S(2)}, u32[]{:S(2)}) %collective-permute-start.5) | collective-permute-done | bytes 208928 | tf_op jit(solution)/shard_map/ppermute | solution.py:191
  122.1 0.0 collective-permute-done.6.refs_7_
  122.1 1.1 shard_map.43
  123.2 17.8 %all_to_all.22 = bf16[8,32,384]{2,1,0:T(8,128)(2,1)S(1)} all-to-all(bf16[8,32,384]{2,1,0:T(8,128)(2,1)S(1)} %bitcast.14), channel_id=1, replica_groups=mesh['x'=4,'zl'=2,'y'=8,'zh'=4,'c'=2] {'zh','zl'}, dimensions={0} | all-to-all | bytes 393216 | tf_op jit(solution)/shard_map/all_to_all | solution.py:174
  141.0 0.7 copy.6
Async XLA Ops:
  6.5 70.7 %all-gather.3.cloned.1.call-start = ((), (), s32[]{:S(2)}) async-start(), calls=%async_computation.4 | async-start | bytes 3538944 | tf_op jit(solution)/shard_map/all_gather | solution.py:202
  49.5 24.3 %all-to-all-start.1 = ((bf16[8,256,384]{2,1,0:T(8,128)(2,1)}), bf16[8,256,384]{2,1,0:T(8,128)(2,1)S(1)}, u32[]{:S(2)}, u32[]{:S(2)}) async-start(bf16[8,256,384]{2,1,0:T(8,128)(2,1)} %broadcast_in_dim.8), calls=%async_computation.1 | async-start | bytes 3145728 | tf_op jit(solution)/shard_map/all_to_all | solution.py:174
  77.2 1.9 %copy-start = (bf16[64,2,32,384]{3,2,1,0:T(8,128)(2,1)S(1)}, bf16[64,2,32,384]{3,2,1,0:T(8,128)(2,1)}, u32[]{:S(2)}) copy-start(bf16[64,2,32,384]{3,2,1,0:T(8,128)(2,1)} %all-gather.3.cloned.1.call-done) | copy-start | bytes 9437188
  83.4 28.2 %collective-permute-start = (bf16[272,384]{1,0:T(8,128)(2,1)S(1)}, bf16[272,384]{1,0:T(8,128)(2,1)S(1)}, u32[]{:S(2)}, u32[]{:S(2)}) collective-permute-start(bf16[272,384]{1,0:T(8,128)(2,1)S(1)} %get-tuple-element.13), channel_id=1, source_target_pairs={{0,256},{1,257},{128,384},{129,385},{256,0},{257,1},{384,128},{385... | collective-permute-start | bytes 626696 | tf_op jit(solution)/shard_map/ppermute | solution.py:191
  86.7 26.7 %collective-permute-start.1 = (bf16[272,384]{1,0:T(8,128)(2,1)S(1)}, bf16[272,384]{1,0:T(8,128)(2,1)S(1)}, u32[]{:S(2)}, u32[]{:S(2)}) collective-permute-start(bf16[272,384]{1,0:T(8,128)(2,1)S(1)} %get-tuple-element.14), channel_id=1, source_target_pairs={{0,257},{1,256},{128,385},{129,384},{256,1},{257,0},{384,129},{385... | collective-permute-start | bytes 626696 | tf_op jit(solution)/shard_map/ppermute | solution.py:191
  93.6 23.3 %collective-permute-start.2 = (bf16[272,384]{1,0:T(8,128)(2,1)S(1)}, bf16[272,384]{1,0:T(8,128)(2,1)S(1)}, u32[]{:S(2)}, u32[]{:S(2)}) collective-permute-start(bf16[272,384]{1,0:T(8,128)(2,1)S(1)} %get-tuple-element.15), channel_id=1, source_target_pairs={{0,128},{1,129},{128,256},{129,257},{256,384},{257,385},{384,0},{3... | collective-permute-start | bytes 626696 | tf_op jit(solution)/shard_map/ppermute | solution.py:191
  96.9 20.0 %collective-permute-start.3 = (bf16[272,384]{1,0:T(8,128)(2,1)S(1)}, bf16[272,384]{1,0:T(8,128)(2,1)S(1)}, u32[]{:S(2)}, u32[]{:S(2)}) collective-permute-start(bf16[272,384]{1,0:T(8,128)(2,1)S(1)} %get-tuple-element.16), channel_id=1, source_target_pairs={{0,129},{1,128},{128,257},{129,256},{256,385},{257,384},{384,1},{3... | collective-permute-start | bytes 626696 | tf_op jit(solution)/shard_map/ppermute | solution.py:191
  104.7 12.2 %collective-permute-start.4 = (bf16[272,384]{1,0:T(8,128)(2,1)S(1)}, bf16[272,384]{1,0:T(8,128)(2,1)S(1)}, u32[]{:S(2)}, u32[]{:S(2)}) collective-permute-start(bf16[272,384]{1,0:T(8,128)(2,1)S(1)} %get-tuple-element.17), channel_id=1, source_target_pairs={{0,384},{1,385},{128,0},{129,1},{256,128},{257,129},{384,256},{385... | collective-permute-start | bytes 626696 | tf_op jit(solution)/shard_map/ppermute | solution.py:191
  111.5 10.5 %collective-permute-start.5 = (bf16[272,384]{1,0:T(8,128)(2,1)S(1)}, bf16[272,384]{1,0:T(8,128)(2,1)S(1)}, u32[]{:S(2)}, u32[]{:S(2)}) collective-permute-start(bf16[272,384]{1,0:T(8,128)(2,1)S(1)} %get-tuple-element.18), channel_id=1, source_target_pairs={{0,385},{1,384},{128,1},{129,0},{256,129},{257,128},{384,257},{385... | collective-permute-start | bytes 626696 | tf_op jit(solution)/shard_map/ppermute | solution.py:191
  113.5 8.6 %collective-permute-start.6 = (bf16[272,384]{1,0:T(8,128)(2,1)S(1)}, bf16[272,384]{1,0:T(8,128)(2,1)S(1)}, u32[]{:S(2)}, u32[]{:S(2)}) collective-permute-start(bf16[272,384]{1,0:T(8,128)(2,1)S(1)} %get-tuple-element.20), channel_id=1, source_target_pairs={{0,1},{1,0},{128,129},{129,128},{256,257},{257,256},{384,385},{385... | collective-permute-start | bytes 626696 | tf_op jit(solution)/shard_map/ppermute | solution.py:191
Sparse Core Ops, SparseCore 0:
  33.6 43.5 all-gather.2

commit v3 on v2

v3 whole, which is shorter than its diff:
```python
import functools
import math

import jax
import jax.numpy as jnp
from jax import lax
from jax.experimental import pallas as pl
from jax.experimental.pallas import tpu as pltpu
from jax.sharding import Mesh, PartitionSpec as P

HEAD_DIM = 128
STAT_ROWS = 16
KEY_CHUNK = 512
EXPONENT = HEAD_DIM**-0.5 * math.log2(math.e)


def head_cols(h):
    return slice(h * HEAD_DIM, (h + 1) * HEAD_DIM)


def attend_kernel(has_state, q_ref, kv_ref, *refs):
    *refs, held_ref, copied, score_a, score_b = refs
    score_refs = (score_a, score_b)
    if has_state:
        sum_ref, stat_ref, out_ref = refs
    else:
        sums_ref, stats_ref = refs
    blocks, rows, width = q_ref.shape
    heads = width // HEAD_DIM
    unit_rows = score_a.shape[0]
    per_unit = unit_rows // rows
    run = held_ref.shape[2]
    step = KEY_CHUNK // run
    chunks = held_ref.shape[0] // step

    def copy(j):
        part = pl.ds(j * step, step)
        return pltpu.make_async_copy(kv_ref.at[part], held_ref.at[part], copied.at[j])

    def kv_chunk(which, h, j):
        block = held_ref[j * step : (j + 1) * step, which, :, head_cols(h)]
        return block.reshape(KEY_CHUNK, HEAD_DIM)

    def query(i, h):
        block = q_ref[i * per_unit : (i + 1) * per_unit, :, head_cols(h)]
        return block.reshape(unit_rows, HEAD_DIM)

    def score_chunk(q, h, slot, j, top):
        s = lax.dot_general(
            q, kv_chunk(0, h, j), (((1,), (1,)), ((), ())), preferred_element_type=jnp.float32
        )
        score_refs[slot][:, j * KEY_CHUNK : (j + 1) * KEY_CHUNK] = s
        for t in range(KEY_CHUNK // HEAD_DIM):
            part = s[:, head_cols(t)]
            top = part if top is None else jnp.maximum(top, part)
        return top

    def span_of(i):
        return slice(i * unit_rows, (i + 1) * unit_rows)

    def shift_of(top, i, h):
        best = jnp.max(top, axis=1, keepdims=True) * EXPONENT
        shift = best.astype(jnp.bfloat16).astype(jnp.float32)
        if has_state:
            shift = jnp.maximum(shift, stat_ref[span_of(i), h : h + 1])
        return shift

    for j in range(chunks):
        copy(j).start()
    work = [(i, h) for i in range(blocks // per_unit) for h in range(heads)]
    lane = lax.broadcasted_iota(jnp.int32, (unit_rows, HEAD_DIM), 1)
    ones = jnp.ones((KEY_CHUNK, HEAD_DIM), jnp.bfloat16)
    top, stats = None, None
    q = query(*work[0])
    for j in range(chunks):
        copy(j).wait()
        top = score_chunk(q, 0, 0, j, top)
    shift = shift_of(top, 0, 0)
    for n, (i, h) in enumerate(work):
        following = work[n + 1] if n + 1 < len(work) else None
        top, total = None, None
        if following:
            q = query(*following)
        for j in range(chunks):
            if following:
                top = score_chunk(q, following[1], (n + 1) % 2, j, top)
            s = score_refs[n % 2][:, j * KEY_CHUNK : (j + 1) * KEY_CHUNK]
            e = jnp.exp2(s * EXPONENT - shift).astype(jnp.bfloat16)
            v = jnp.concatenate([kv_chunk(1, h, j), ones], axis=1)
            o = jnp.dot(e, v, preferred_element_type=jnp.float32)
            total = o if total is None else total + o
        sums, denom = total[:, 0:HEAD_DIM], total[:, HEAD_DIM:]
        span = span_of(i)
        if h == 0:
            stats = jnp.zeros((unit_rows, HEAD_DIM), jnp.float32)
        stats = jnp.where(lane == h, shift, stats)
        if has_state:
            factor = jnp.exp2(stat_ref[span, h : h + 1] - shift)
            sums = sums + factor * sum_ref[span, head_cols(h)]
            denom = denom + factor * stat_ref[span, heads + h : heads + h + 1]
            for b in range(per_unit):
                part = sums[b * rows : (b + 1) * rows].astype(jnp.bfloat16)
                out_ref[i * per_unit + b, 0:rows, head_cols(h)] = part
            high = denom.astype(jnp.bfloat16).astype(jnp.float32)
            stats = jnp.where(lane == heads + h, high, stats)
            stats = jnp.where(lane == 2 * heads + h, denom - high, stats)
        else:
            sums_ref[span, head_cols(h)] = sums
            stats = jnp.where(lane == heads + h, denom, stats)
        if h + 1 == heads:
            if has_state:
                flipped = stats.T[0:STAT_ROWS].astype(jnp.bfloat16)
                blank = jnp.zeros((STAT_ROWS, width - rows), jnp.bfloat16)
                for b in range(per_unit):
                    block = i * per_unit + b
                    out_ref[block, rows:, 0:rows] = flipped[:, b * rows : (b + 1) * rows]
                    out_ref[block, rows:, rows:] = blank
            else:
                stats_ref[span, :] = stats
        if following:
            shift = shift_of(top, *following)


def attend(q, kv, state=None):
    blocks, rows, width = q.shape
    heads = width // HEAD_DIM
    keys_n = kv.shape[0] * kv.shape[2]
    vmem = pl.BlockSpec(memory_space=pltpu.VMEM)
    if state:
        out_shape = jax.ShapeDtypeStruct((blocks, rows + STAT_ROWS, width), jnp.bfloat16)
        out_specs = vmem
    else:
        out_shape = [
            jax.ShapeDtypeStruct((blocks * rows, width), jnp.float32),
            jax.ShapeDtypeStruct((blocks * rows, HEAD_DIM), jnp.float32),
        ]
        out_specs = [vmem, vmem]
    state = state or []
    unit_rows = 2 * rows
    return pl.pallas_call(
        functools.partial(attend_kernel, bool(state)),
        in_specs=[vmem, pl.BlockSpec(memory_space=pl.ANY)] + [vmem] * len(state),
        out_specs=out_specs,
        out_shape=out_shape,
        scratch_shapes=[
            pltpu.VMEM(kv.shape, kv.dtype),
            pltpu.SemaphoreType.DMA((keys_n // KEY_CHUNK,)),
            pltpu.VMEM((unit_rows, keys_n), jnp.float32),
            pltpu.VMEM((unit_rows, keys_n), jnp.float32),
        ],
        compiler_params=pltpu.CompilerParams(vmem_limit_bytes=36 * 2**20),
        cost_estimate=pl.CostEstimate(
            flops=4 * blocks * rows * keys_n * width,
            bytes_accessed=4 * (blocks * rows * width + keys_n * width),
            transcendentals=blocks * rows * keys_n * heads,
        ),
    )(q, kv, *state)


def merge_kernel(parts_ref, out_ref):
    pieces = parts_ref.shape[0]
    rows, width = out_ref.shape
    heads = width // HEAD_DIM
    stats = [
        parts_ref[p, rows : rows + STAT_ROWS, 0:rows].astype(jnp.float32) for p in range(pieces)
    ]
    shifts = [s[0:heads] for s in stats]
    totals = [s[heads : 2 * heads] + s[2 * heads : 3 * heads] for s in stats]
    best = functools.reduce(jnp.maximum, shifts)
    factors = [jnp.exp2(s - best) for s in shifts]
    denom = sum(f * t for f, t in zip(factors, totals))
    weights = jnp.concatenate([f / denom for f in factors], axis=0)
    pad = jnp.zeros((HEAD_DIM - weights.shape[0], rows), jnp.float32)
    weights = jnp.concatenate([weights, pad], axis=0).T
    for h in range(heads):
        total = jnp.zeros((rows, HEAD_DIM), jnp.float32)
        for p in range(pieces):
            w = weights[:, p * heads + h : p * heads + h + 1]
            total = total + w * parts_ref[p, 0:rows, head_cols(h)].astype(jnp.float32)
        out_ref[:, head_cols(h)] = total.astype(jnp.bfloat16)


def merge(parts):
    pieces, part_rows, width = parts.shape
    return pl.pallas_call(
        merge_kernel,
        out_shape=jax.ShapeDtypeStruct((part_rows - STAT_ROWS, width), jnp.bfloat16),
        in_specs=[pl.BlockSpec(memory_space=pltpu.VMEM)],
        out_specs=pl.BlockSpec(memory_space=pltpu.VMEM),
        compiler_params=pltpu.CompilerParams(vmem_limit_bytes=32 * 2**20),
    )(parts)


def split_kernel(*refs):
    *in_refs, out_ref = refs
    groups, arrays, rows, width = out_ref.shape
    for g in range(groups):
        for a in range(arrays):
            out_ref[g, a] = in_refs[a][:, g * width : (g + 1) * width]


def split(groups, *arrays):
    rows, columns = arrays[0].shape
    return pl.pallas_call(
        split_kernel,
        out_shape=jax.ShapeDtypeStruct(
            (groups, len(arrays), rows, columns // groups), arrays[0].dtype
        ),
        in_specs=[pl.BlockSpec(memory_space=pltpu.VMEM)] * len(arrays),
        out_specs=pl.BlockSpec(memory_space=pltpu.VMEM),
    )(*arrays)


HEAD_AXES = ("zh", "zl")
KEY_AXES = ("y",)
ROW_AXES = ("x",)
ALL_AXES = ("x", "zl", "y", "zh", "c")


def exchange(array, axes):
    return lax.all_to_all(array, axes, split_axis=0, concat_axis=0, tiled=True)


def shards(queries, keys, values):
    groups = lax.axis_size(HEAD_AXES)
    blocks = lax.axis_size(ROW_AXES)
    rows, columns = queries.shape
    width = columns // groups
    kv = exchange(split(groups, keys, values), HEAD_AXES)
    kv = lax.all_gather(kv, KEY_AXES, axis=0, tiled=True)
    q = exchange(split(groups, queries), HEAD_AXES).reshape(1, groups * rows, width)
    q = exchange(jnp.broadcast_to(q, (blocks, groups * rows, width)), ROW_AXES)
    kv, q = lax.optimization_barrier((kv, q))
    other_kv = lax.ppermute(kv, "c", [(0, 1), (1, 0)])
    parts = attend(q, other_kv, attend(q, kv))
    merged = merge(exchange(parts, ROW_AXES)).reshape(groups, rows, width)
    spread = exchange(merged, HEAD_AXES)
    return spread.transpose(1, 0, 2).reshape(rows, columns)


def solution(mesh):
    fine = Mesh(mesh.devices.reshape(4, 2, 8, 4, 2), ALL_AXES)
    placed = P(ALL_AXES, None)
    return jax.shard_map(
        shards, mesh=fine, in_specs=(placed,) * 3, out_specs=placed, check_vma=False
    )
```

time: 149 us -> 142 us (0.953)
  blocking collectives: 56 us -> 83.4 us
  starting transfers between devices: 25.4 us -> 1.91 us
  waiting for transfers between devices: 27.8 us -> 16.7 us
    all_to_all x3 -> x5, blocking collectives: 56 us -> 83.4 us  [exchange(): return lax.all_to_all(array, axes, split_axis=0, concat_axis=0, tiled=True)]
    all_to_all x1 -> x0, waiting for transfers between devices: 19.2 us -> none  [exchange(): return lax.all_to_all(array, axes, split_axis=0, concat_axis=0, tiled=True)]
    ppermute x7 -> x1, starting transfers between devices: 20.7 us -> 1.91 us  [shards(): other_kv = lax.ppermute(kv, 'c', [(0, 1), (1, 0)])]
    all_gather x1, waiting for transfers between devices: 3.43 us -> 16.7 us  [shards(): kv = lax.all_gather(kv, KEY_AXES, axis=0, tiled=True)]
    ppermute x7 -> x1, waiting for transfers between devices: 5.15 us -> 0.01 us  [shards(): other_kv = lax.ppermute(kv, 'c', [(0, 1), (1, 0)])]
    all_to_all x1 -> x0, starting transfers between devices: 4.78 us -> none  [exchange(): return lax.all_to_all(array, axes, split_axis=0, concat_axis=0, tiled=True)]
    pallas_call x4 -> x2, Pallas kernels: 17.1 us -> 18.1 us  [attend(): pl.pallas_call(functools.partial(attend_kernel, bool(state)), in_specs=[v...]
  transfers between devices with their start and end apart: 9 -> 2, of which waited for: 3 -> 1; matrix products, arithmetic and copies ran while one was open for 1% -> 0% of each run, Pallas kernels for 10% -> 7%
where the time goes in v3:
time: 142 us; the launch traced here: 140 us
  blocking collectives  83.4 us (59%)
  Pallas kernels  22.1 us (16%)
  waiting for transfers between devices  16.7 us (12%)
  between operations  13.4 us (9%)
  local copies, waits for them, and re-layouts  2.65 us (2%)
  starting transfers between devices  1.91 us (1%)
    all_to_all x5, blocking collectives, exchange(): return lax.all_to_all(array, axes, split_axis=0, concat_axis=0, tiled=True)  83.4 us
    pallas_call x2, Pallas kernels, attend(): pl.pallas_call(functools.partial(attend_kernel, bool(state)), in_specs=[v...  18.1 us
    all_gather x1, waiting for transfers between devices, shards(): kv = lax.all_gather(kv, KEY_AXES, axis=0, tiled=True)  16.7 us
    pallas_call x2, Pallas kernels, split(): pl.pallas_call(split_kernel, out_shape=jax.ShapeDtypeStruct((groups, len(...  3.42 us
  transfers between devices with their start and end apart: 2, of which 1 were waited for; matrix products, arithmetic and copies ran while one was open for 0% of the time, Pallas kernels for 7%

profile of v3, /device:TPU:6, one launch (start us, length us, event | category | flops | bytes accessed | tf_op | source)
XLA Modules:
  0.0 140.2 jit_solution(10498950868189029485)
XLA Ops:
  6.5 0.0 all-gather.2.cloned.1.call-start
  6.5 1.8 %shard_map.37 = bf16[8,2,32,384]{3,2,1,0:T(8,128)(2,1)} custom-call(bf16[32,3072]{1,0:T(8,128)(2,1)} %refs_0_.2, bf16[32,3072]{1,0:T(8,128)(2,1)} %refs_1_.1), custom_call_target="tpu_custom_call" | custom-call | tf_op jit(solution)/shard_map/pallas_call | solution.py:204
  8.3 25.1 %all_to_all.25 = bf16[8,2,32,384]{3,2,1,0:T(8,128)(2,1)} all-to-all(bf16[8,2,32,384]{3,2,1,0:T(8,128)(2,1)} %shard_map.37), channel_id=1, replica_groups=mesh['x'=4,'zl'=2,'y'=8,'zh'=4,'c'=2] {'zh','zl'}, dimensions={0} | all-to-all | bytes 786432 | tf_op jit(solution)/shard_map/all_to_all | solution.py:221
  33.4 0.0 all-gather.2.cloned.1.call-update
  33.5 1.6 %shard_map.38 = bf16[8,1,32,384]{3,2,1,0:T(8,128)(2,1)} custom-call(bf16[32,3072]{1,0:T(8,128)(2,1)} %refs_0_.3), custom_call_target="tpu_custom_call" | custom-call | tf_op jit(solution)/shard_map/pallas_call | solution.py:204
  35.1 13.1 %all_to_all.26 = bf16[8,1,32,384]{3,2,1,0:T(8,128)(2,1)S(1)} all-to-all(bf16[8,1,32,384]{3,2,1,0:T(8,128)(2,1)} %shard_map.38), channel_id=1, replica_groups=mesh['x'=4,'zl'=2,'y'=8,'zh'=4,'c'=2] {'zh','zl'}, dimensions={0} | all-to-all | bytes 393216 | tf_op jit(solution)/shard_map/all_to_all | solution.py:221
  48.2 0.1 broadcast_in_dim.8
  48.2 12.2 %all_to_all.27.q_ref = bf16[4,256,384]{2,1,0:T(8,128)(2,1)S(1)} all-to-all(bf16[4,256,384]{2,1,0:T(8,128)(2,1)S(1)} %broadcast_in_dim.8), channel_id=1, replica_groups=mesh['x'=4,'zl'=2,'y'=8,'zh'=4,'c'=2] {'x'}, dimensions={0} | all-to-all | bytes 1572864 | tf_op jit(solution)/shard_map/all_to_all | solution.py:221
  60.5 16.7 %all-gather.2.cloned.1.call-done.kv_ref = bf16[64,2,32,384]{3,2,1,0:T(8,128)(2,1)} async-done(((bf16[8,2,32,384]{3,2,1,0:T(8,128)(2,1)}), bf16[64,2,32,384]{3,2,1,0:T(8,128)(2,1)}) %all-gather.2.cloned.1.call-update) | async-done | bytes 3145744 | tf_op jit(solution)/shard_map/all_gather | solution.py:230
  77.2 1.9 %collective-permute-start = (bf16[64,2,32,384]{3,2,1,0:T(8,128)(2,1)}, bf16[64,2,32,384]{3,2,1,0:T(8,128)(2,1)S(1)}, u32[]{:S(2)}, u32[]{:S(2)}) collective-permute-start(bf16[64,2,32,384]{3,2,1,0:T(8,128)(2,1)} %all-gather.2.cloned.1.call-done.kv_ref), channel_id=1, source_target_pairs={{0,1},{1,0},{2,3},{3,2},{4,5},{5,4},{6,7},{7,6},{8,9},{9,8},{10,11... | collective-permute-start | bytes 9437192 | tf_op jit(solution)/shard_map/ppermute | solution.py:234
  79.1 0.0 copy-start
  79.1 1.9 %copy-done = bf16[64,2,32,384]{3,2,1,0:T(8,128)(2,1)S(1)} copy-done((bf16[64,2,32,384]{3,2,1,0:T(8,128)(2,1)S(1)}, bf16[64,2,32,384]{3,2,1,0:T(8,128)(2,1)}, u32[]{:S(2)}) %copy-start) | copy-done | bytes 3145752
  81.0 8.3 %shard_map.39 = (f32[1024,384]{1,0:T(8,128)S(1)}, f32[1024,128]{1,0:T(8,128)S(1)}) custom-call(bf16[4,256,384]{2,1,0:T(8,128)(2,1)S(1)} %all_to_all.27.q_ref, bf16[64,2,32,384]{3,2,1,0:T(8,128)(2,1)S(1)} %copy-done), custom_call_target="tpu_custom_call" | custom-call | flops 3221225472 | bytes 4718592 | tf_op jit(solution)/shard_map/pallas_call | solution.py:140
  89.3 0.0 collective-permute-done.kv_ref
  89.3 9.7 %shard_map.40 = bf16[4,272,384]{2,1,0:T(8,128)(2,1)S(1)} custom-call(bf16[4,256,384]{2,1,0:T(8,128)(2,1)S(1)} %all_to_all.27.q_ref, bf16[64,2,32,384]{3,2,1,0:T(8,128)(2,1)S(1)} %collective-permute-done.kv_ref, f32[1024,384]{1,0:T(8,128)S(1)} %get-tuple-element.11.refs_0_, f32[1024,128]{1,0:T(8,128)S(1)} %get-tuple-element.12.refs_1_), custom_call_target="tpu_custom_call" | custom-call | flops 3221225472 | bytes 4718592 | tf_op jit(solution)/shard_map/pallas_call | solution.py:140
  99.1 16.0 %all_to_all.28.parts_ref = bf16[4,272,384]{2,1,0:T(8,128)(2,1)S(1)} all-to-all(bf16[4,272,384]{2,1,0:T(8,128)(2,1)S(1)} %shard_map.40), channel_id=1, replica_groups=mesh['x'=4,'zl'=2,'y'=8,'zh'=4,'c'=2] {'x'}, dimensions={0} | all-to-all | bytes 1671168 | tf_op jit(solution)/shard_map/all_to_all | solution.py:221
  115.1 0.6 shard_map.41
  115.7 17.0 %all_to_all.29 = bf16[8,32,384]{2,1,0:T(8,128)(2,1)S(1)} all-to-all(bf16[8,32,384]{2,1,0:T(8,128)(2,1)S(1)} %bitcast.5), channel_id=1, replica_groups=mesh['x'=4,'zl'=2,'y'=8,'zh'=4,'c'=2] {'zh','zl'}, dimensions={0} | all-to-all | bytes 393216 | tf_op jit(solution)/shard_map/all_to_all | solution.py:221
  132.7 0.7 copy.6
Async XLA Ops:
  6.5 70.6 %all-gather.2.cloned.1.call-start = ((), (), s32[]{:S(2)}) async-start(), calls=%async_computation.5 | async-start | bytes 3538944 | tf_op jit(solution)/shard_map/all_gather | solution.py:230
  77.2 12.2 %collective-permute-start = (bf16[64,2,32,384]{3,2,1,0:T(8,128)(2,1)}, bf16[64,2,32,384]{3,2,1,0:T(8,128)(2,1)S(1)}, u32[]{:S(2)}, u32[]{:S(2)}) collective-permute-start(bf16[64,2,32,384]{3,2,1,0:T(8,128)(2,1)} %all-gather.2.cloned.1.call-done.kv_ref), channel_id=1, source_target_pairs={{0,1},{1,0},{2,3},{3,2},{4,5},{5,4},{6,7},{7,6},{8,9},{9,8},{10,11... | collective-permute-start | bytes 9437192 | tf_op jit(solution)/shard_map/ppermute | solution.py:234
  79.1 1.9 %copy-start = (bf16[64,2,32,384]{3,2,1,0:T(8,128)(2,1)S(1)}, bf16[64,2,32,384]{3,2,1,0:T(8,128)(2,1)}, u32[]{:S(2)}) copy-start(bf16[64,2,32,384]{3,2,1,0:T(8,128)(2,1)} %all-gather.2.cloned.1.call-done.kv_ref) | copy-start | bytes 9437188
Sparse Core Ops, SparseCore 0:
  33.6 43.5 all-gather.1

commit v4 on v3

--- a/solution.py
+++ b/solution.py
@@ -139,7 +139,7 @@
     unit_rows = 2 * rows
     return pl.pallas_call(
         functools.partial(attend_kernel, bool(state)),
-        in_specs=[vmem, pl.BlockSpec(memory_space=pl.ANY)] + [vmem] * len(state),
+        in_specs=[vmem, pl.BlockSpec(memory_space=pl.ANY if state else pltpu.HBM)] + [vmem] * len(state),
         out_specs=out_specs,
         out_shape=out_shape,
         scratch_shapes=[
@@ -211,9 +211,9 @@
     )(*arrays)
 
 
-HEAD_AXES = ("zh", "zl")
+HEAD_AXES = ("x", "zl")
 KEY_AXES = ("y",)
-ROW_AXES = ("x",)
+ROW_AXES = ("zh",)
 ALL_AXES = ("x", "zl", "y", "zh", "c")
 
 

time: 142 us -> 146 us (1.028)
  blocking collectives: 83.4 us -> 93.9 us
  waiting for transfers between devices: 16.7 us -> 9.99 us
    all_to_all x5, blocking collectives: 83.4 us -> 93.9 us  [exchange(): return lax.all_to_all(array, axes, split_axis=0, concat_axis=0, tiled=True)]
    all_gather x1, waiting for transfers between devices: 16.7 us -> 9.97 us  [shards(): kv = lax.all_gather(kv, KEY_AXES, axis=0, tiled=True)]
where the time goes in v4:
time: 146 us; the launch traced here: 144 us
  blocking collectives  93.9 us (64%)
  Pallas kernels  22.1 us (15%)
  between operations  13.4 us (9%)
  waiting for transfers between devices  9.99 us (7%)
  local copies, waits for them, and re-layouts  2.65 us (2%)
  starting transfers between devices  1.91 us (1%)
    all_to_all x5, blocking collectives, exchange(): return lax.all_to_all(array, axes, split_axis=0, concat_axis=0, tiled=True)  93.9 us
    pallas_call x2, Pallas kernels, attend(): pl.pallas_call(functools.partial(attend_kernel, bool(state)), in_specs=[v...  18.1 us
    all_gather x1, waiting for transfers between devices, shards(): kv = lax.all_gather(kv, KEY_AXES, axis=0, tiled=True)  9.97 us
    pallas_call x2, Pallas kernels, split(): pl.pallas_call(split_kernel, out_shape=jax.ShapeDtypeStruct((groups, len(...  3.42 us
  transfers between devices with their start and end apart: 2, of which 1 were waited for; matrix products, arithmetic and copies ran while one was open for 0% of the time, Pallas kernels for 7%

profile of v4, /device:TPU:6, one launch (start us, length us, event | category | flops | bytes accessed | tf_op | source)
XLA Modules:
  0.0 144.0 jit_solution(4196156154953216255)
XLA Ops:
  6.5 0.0 all-gather.2.cloned.1.call-start
  6.5 1.8 %shard_map.37 = bf16[8,2,32,384]{3,2,1,0:T(8,128)(2,1)} custom-call(bf16[32,3072]{1,0:T(8,128)(2,1)} %refs_0_.2, bf16[32,3072]{1,0:T(8,128)(2,1)} %refs_1_.1), custom_call_target="tpu_custom_call" | custom-call | tf_op jit(solution)/shard_map/pallas_call | solution.py:204
  8.3 15.8 %all_to_all.25 = bf16[8,2,32,384]{3,2,1,0:T(8,128)(2,1)} all-to-all(bf16[8,2,32,384]{3,2,1,0:T(8,128)(2,1)} %shard_map.37), channel_id=1, replica_groups=mesh['x'=4,'zl'=2,'y'=8,'zh'=4,'c'=2] {'x','zl'}, dimensions={0} | all-to-all | bytes 786432 | tf_op jit(solution)/shard_map/all_to_all | solution.py:221
  24.1 0.0 all-gather.2.cloned.1.call-update
  24.1 1.6 %shard_map.38 = bf16[8,1,32,384]{3,2,1,0:T(8,128)(2,1)} custom-call(bf16[32,3072]{1,0:T(8,128)(2,1)} %refs_0_.3), custom_call_target="tpu_custom_call" | custom-call | tf_op jit(solution)/shard_map/pallas_call | solution.py:204
  25.8 10.2 %all_to_all.26 = bf16[8,1,32,384]{3,2,1,0:T(8,128)(2,1)S(1)} all-to-all(bf16[8,1,32,384]{3,2,1,0:T(8,128)(2,1)} %shard_map.38), channel_id=1, replica_groups=mesh['x'=4,'zl'=2,'y'=8,'zh'=4,'c'=2] {'x','zl'}, dimensions={0} | all-to-all | bytes 393216 | tf_op jit(solution)/shard_map/all_to_all | solution.py:221
  35.9 0.1 broadcast_in_dim.8
  36.0 26.8 %all_to_all.27.q_ref = bf16[4,256,384]{2,1,0:T(8,128)(2,1)S(1)} all-to-all(bf16[4,256,384]{2,1,0:T(8,128)(2,1)S(1)} %broadcast_in_dim.8), channel_id=1, replica_groups=mesh['x'=4,'zl'=2,'y'=8,'zh'=4,'c'=2] {'zh'}, dimensions={0} | all-to-all | bytes 1572864 | tf_op jit(solution)/shard_map/all_to_all | solution.py:221
  62.8 10.0 %all-gather.2.cloned.1.call-done.kv_ref = bf16[64,2,32,384]{3,2,1,0:T(8,128)(2,1)} async-done(((bf16[8,2,32,384]{3,2,1,0:T(8,128)(2,1)}), bf16[64,2,32,384]{3,2,1,0:T(8,128)(2,1)}) %all-gather.2.cloned.1.call-update) | async-done | bytes 3145744 | tf_op jit(solution)/shard_map/all_gather | solution.py:230
  72.8 1.9 %collective-permute-start = (bf16[64,2,32,384]{3,2,1,0:T(8,128)(2,1)}, bf16[64,2,32,384]{3,2,1,0:T(8,128)(2,1)S(1)}, u32[]{:S(2)}, u32[]{:S(2)}) collective-permute-start(bf16[64,2,32,384]{3,2,1,0:T(8,128)(2,1)} %all-gather.2.cloned.1.call-done.kv_ref), channel_id=1, source_target_pairs={{0,1},{1,0},{2,3},{3,2},{4,5},{5,4},{6,7},{7,6},{8,9},{9,8},{10,11... | collective-permute-start | bytes 9437192 | tf_op jit(solution)/shard_map/ppermute | solution.py:234
  74.7 0.0 copy-start
  74.7 1.9 %copy-done = bf16[64,2,32,384]{3,2,1,0:T(8,128)(2,1)S(1)} copy-done((bf16[64,2,32,384]{3,2,1,0:T(8,128)(2,1)S(1)}, bf16[64,2,32,384]{3,2,1,0:T(8,128)(2,1)}, u32[]{:S(2)}) %copy-start) | copy-done | bytes 3145752
  76.6 8.3 %shard_map.39 = (f32[1024,384]{1,0:T(8,128)S(1)}, f32[1024,128]{1,0:T(8,128)S(1)}) custom-call(bf16[4,256,384]{2,1,0:T(8,128)(2,1)S(1)} %all_to_all.27.q_ref, bf16[64,2,32,384]{3,2,1,0:T(8,128)(2,1)S(1)} %copy-done), custom_call_target="tpu_custom_call" | custom-call | flops 3221225472 | bytes 4718592 | tf_op jit(solution)/shard_map/pallas_call | solution.py:140
  85.0 0.0 collective-permute-done.kv_ref
  85.0 9.7 %shard_map.40 = bf16[4,272,384]{2,1,0:T(8,128)(2,1)S(1)} custom-call(bf16[4,256,384]{2,1,0:T(8,128)(2,1)S(1)} %all_to_all.27.q_ref, bf16[64,2,32,384]{3,2,1,0:T(8,128)(2,1)S(1)} %collective-permute-done.kv_ref, f32[1024,384]{1,0:T(8,128)S(1)} %get-tuple-element.11.refs_0_, f32[1024,128]{1,0:T(8,128)S(1)} %get-tuple-element.12.refs_1_), custom_call_target="tpu_custom_call" | custom-call | flops 3221225472 | bytes 4718592 | tf_op jit(solution)/shard_map/pallas_call | solution.py:140
  94.7 31.1 %all_to_all.28.parts_ref = bf16[4,272,384]{2,1,0:T(8,128)(2,1)S(1)} all-to-all(bf16[4,272,384]{2,1,0:T(8,128)(2,1)S(1)} %shard_map.40), channel_id=1, replica_groups=mesh['x'=4,'zl'=2,'y'=8,'zh'=4,'c'=2] {'zh'}, dimensions={0} | all-to-all | bytes 1671168 | tf_op jit(solution)/shard_map/all_to_all | solution.py:221
  125.8 0.6 shard_map.41
  126.4 10.0 %all_to_all.29 = bf16[8,32,384]{2,1,0:T(8,128)(2,1)S(1)} all-to-all(bf16[8,32,384]{2,1,0:T(8,128)(2,1)S(1)} %bitcast.5), channel_id=1, replica_groups=mesh['x'=4,'zl'=2,'y'=8,'zh'=4,'c'=2] {'x','zl'}, dimensions={0} | all-to-all | bytes 393216 | tf_op jit(solution)/shard_map/all_to_all | solution.py:221
  136.4 0.7 copy.6
Async XLA Ops:
  6.5 66.3 %all-gather.2.cloned.1.call-start = ((), (), s32[]{:S(2)}) async-start(), calls=%async_computation.5 | async-start | bytes 3538944 | tf_op jit(solution)/shard_map/all_gather | solution.py:230
  72.8 12.2 %collective-permute-start = (bf16[64,2,32,384]{3,2,1,0:T(8,128)(2,1)}, bf16[64,2,32,384]{3,2,1,0:T(8,128)(2,1)S(1)}, u32[]{:S(2)}, u32[]{:S(2)}) collective-permute-start(bf16[64,2,32,384]{3,2,1,0:T(8,128)(2,1)} %all-gather.2.cloned.1.call-done.kv_ref), channel_id=1, source_target_pairs={{0,1},{1,0},{2,3},{3,2},{4,5},{5,4},{6,7},{7,6},{8,9},{9,8},{10,11... | collective-permute-start | bytes 9437192 | tf_op jit(solution)/shard_map/ppermute | solution.py:234
  74.7 1.9 %copy-start = (bf16[64,2,32,384]{3,2,1,0:T(8,128)(2,1)S(1)}, bf16[64,2,32,384]{3,2,1,0:T(8,128)(2,1)}, u32[]{:S(2)}) copy-start(bf16[64,2,32,384]{3,2,1,0:T(8,128)(2,1)} %all-gather.2.cloned.1.call-done.kv_ref) | copy-start | bytes 9437188
Sparse Core Ops, SparseCore 0:
  24.3 48.4 all-gather.1

commit v5 on v3

v5 whole, which is shorter than its diff:
```python
import functools
import math

import jax
import jax.numpy as jnp
from jax import lax
from jax.experimental import pallas as pl
from jax.experimental.pallas import tpu as pltpu
from jax.sharding import Mesh, PartitionSpec as P

HEAD_DIM = 128
STAT_ROWS = 16
KEY_CHUNK = 512
EXPONENT = HEAD_DIM**-0.5 * math.log2(math.e)


def head_cols(h):
    return slice(h * HEAD_DIM, (h + 1) * HEAD_DIM)


def attend_kernel(at_ref, q_ref, kv_ref, *refs):
    *out_refs, held_ref, copied, score_a, score_b = refs
    score_refs = (score_a, score_b)
    blocks, rows, width = q_ref.shape
    heads = width // HEAD_DIM
    unit_rows = score_a.shape[0]
    per_unit = unit_rows // rows
    run = held_ref.shape[2]
    step = KEY_CHUNK // run
    chunks = held_ref.shape[0] // step

    def copy(which, j):
        part = pl.ds(j * step, step)
        return pltpu.make_async_copy(
            kv_ref.at[part, which], held_ref.at[part, which], copied.at[which, j]
        )

    def kv_chunk(which, h, j):
        block = held_ref[j * step : (j + 1) * step, which, :, head_cols(h)]
        return block.reshape(KEY_CHUNK, HEAD_DIM)

    def query(i, h):
        parts = [q_ref[at_ref[i * per_unit + b], :, head_cols(h)] for b in range(per_unit)]
        return jnp.concatenate(parts, axis=0)

    def cols_of(j):
        return slice(j * KEY_CHUNK, (j + 1) * KEY_CHUNK)

    def score_chunk(q, h, slot, j, top):
        s = lax.dot_general(
            q, kv_chunk(0, h, j), (((1,), (1,)), ((), ())), preferred_element_type=jnp.float32
        )
        score_refs[slot][:, cols_of(j)] = s
        for t in range(KEY_CHUNK // HEAD_DIM):
            part = s[:, head_cols(t)]
            top = part if top is None else jnp.maximum(top, part)
        return top

    def shift_of(top):
        best = jnp.max(top, axis=1, keepdims=True) * EXPONENT
        return best.astype(jnp.bfloat16).astype(jnp.float32)

    for which in range(2):
        for j in range(chunks):
            copy(which, j).start()
    work = [(i, h) for i in range(blocks // per_unit) for h in range(heads)]
    lane = lax.broadcasted_iota(jnp.int32, (unit_rows, HEAD_DIM), 1)
    ones = jnp.ones((KEY_CHUNK, HEAD_DIM), jnp.bfloat16)
    top, stats = None, None
    q = query(*work[0])
    for j in range(chunks):
        copy(0, j).wait()
        top = score_chunk(q, 0, 0, j, top)
    shift = shift_of(top)
    for n, (i, h) in enumerate(work):
        following = work[n + 1] if n + 1 < len(work) else None
        top, total = None, None
        if following:
            q = query(*following)
        for j in range(chunks):
            if following:
                top = score_chunk(q, following[1], (n + 1) % 2, j, top)
            s = score_refs[n % 2][:, cols_of(j)]
            e = jnp.exp2(s * EXPONENT - shift).astype(jnp.bfloat16)
            if n == 0:
                copy(1, j).wait()
            v = jnp.concatenate([kv_chunk(1, h, j), ones], axis=1)
            o = jnp.dot(e, v, preferred_element_type=jnp.float32)
            total = o if total is None else total + o
        sums, denom = total[:, 0:HEAD_DIM], total[:, HEAD_DIM:]
        for b in range(per_unit):
            part = sums[b * rows : (b + 1) * rows].astype(jnp.bfloat16)
            out_refs[i * per_unit + b][0:rows, head_cols(h)] = part
        if h == 0:
            stats = jnp.zeros((unit_rows, HEAD_DIM), jnp.float32)
        high = denom.astype(jnp.bfloat16).astype(jnp.float32)
        stats = jnp.where(lane == h, shift, stats)
        stats = jnp.where(lane == heads + h, high, stats)
        stats = jnp.where(lane == 2 * heads + h, denom - high, stats)
        if h + 1 == heads:
            flipped = stats.T[0:STAT_ROWS].astype(jnp.bfloat16)
            blank = jnp.zeros((STAT_ROWS, width - rows), jnp.bfloat16)
            for b in range(per_unit):
                out_ref = out_refs[i * per_unit + b]
                out_ref[rows:, 0:rows] = flipped[:, b * rows : (b + 1) * rows]
                out_ref[rows:, rows:] = blank
        if following:
            shift = shift_of(top)


def attend(at, q, kv):
    blocks, rows, width = q.shape
    heads = width // HEAD_DIM
    keys_n = kv.shape[0] * kv.shape[2]
    vmem = pl.BlockSpec(memory_space=pltpu.VMEM)
    unit_rows = 2 * rows
    return pl.pallas_call(
        attend_kernel,
        in_specs=[
            pl.BlockSpec(memory_space=pltpu.SMEM),
            vmem,
            pl.BlockSpec(memory_space=pl.ANY),
        ],
        out_specs=[vmem] * blocks,
        out_shape=[jax.ShapeDtypeStruct((rows + STAT_ROWS, width), jnp.bfloat16)] * blocks,
        scratch_shapes=[
            pltpu.VMEM(kv.shape, kv.dtype),
            pltpu.SemaphoreType.DMA((2, keys_n // KEY_CHUNK)),
            pltpu.VMEM((unit_rows, keys_n), jnp.float32),
            pltpu.VMEM((unit_rows, keys_n), jnp.float32),
        ],
        compiler_params=pltpu.CompilerParams(vmem_limit_bytes=56 * 2**20),
        cost_estimate=pl.CostEstimate(
            flops=4 * blocks * rows * keys_n * width,
            bytes_accessed=4 * (blocks * rows * width + keys_n * width),
            transcendentals=blocks * rows * keys_n * heads,
        ),
    )(at, q, kv)


def merge_kernel(*refs):
    *part_refs, out_ref = refs
    rows, width = out_ref.shape
    heads = width // HEAD_DIM
    stats = [
        ref[rows : rows + STAT_ROWS, 0:rows].astype(jnp.float32) for ref in part_refs
    ]
    shifts = [s[0:heads] for s in stats]
    totals = [s[heads : 2 * heads] + s[2 * heads : 3 * heads] for s in stats]
    best = functools.reduce(jnp.maximum, shifts)
    factors = [jnp.exp2(s - best) for s in shifts]
    denom = sum(f * t for f, t in zip(factors, totals))
    weights = jnp.concatenate([f / denom for f in factors], axis=0)
    pad = jnp.zeros((HEAD_DIM - weights.shape[0], rows), jnp.float32)
    weights = jnp.concatenate([weights, pad], axis=0).T
    for h in range(heads):
        total = jnp.zeros((rows, HEAD_DIM), jnp.float32)
        for p, ref in enumerate(part_refs):
            w = weights[:, p * heads + h : p * heads + h + 1]
            total = total + w * ref[0:rows, head_cols(h)].astype(jnp.float32)
        out_ref[:, head_cols(h)] = total.astype(jnp.bfloat16)


def merge(parts):
    part_rows, width = parts[0].shape
    return pl.pallas_call(
        merge_kernel,
        out_shape=jax.ShapeDtypeStruct((part_rows - STAT_ROWS, width), jnp.bfloat16),
        in_specs=[pl.BlockSpec(memory_space=pltpu.VMEM)] * len(parts),
        out_specs=pl.BlockSpec(memory_space=pltpu.VMEM),
        compiler_params=pltpu.CompilerParams(vmem_limit_bytes=32 * 2**20),
    )(*parts)


def split_kernel(*refs):
    *in_refs, out_ref = refs
    groups, arrays, rows, width = out_ref.shape
    for g in range(groups):
        for a in range(arrays):
            out_ref[g, a] = in_refs[a][:, g * width : (g + 1) * width]


def split(groups, *arrays):
    rows, columns = arrays[0].shape
    return pl.pallas_call(
        split_kernel,
        out_shape=jax.ShapeDtypeStruct(
            (groups, len(arrays), rows, columns // groups), arrays[0].dtype
        ),
        in_specs=[pl.BlockSpec(memory_space=pltpu.VMEM)] * len(arrays),
        out_specs=pl.BlockSpec(memory_space=pltpu.VMEM),
    )(*arrays)


HEAD_AXES = ("zh", "zl")
KEY_AXES = ("y", "c")
ROW_AXES = ("x",)
ALL_AXES = ("x", "zl", "y", "zh", "c")


def exchange(array, axes):
    return lax.all_to_all(array, axes, split_axis=0, concat_axis=0, tiled=True)


def shards(queries, keys, values):
    groups = lax.axis_size(HEAD_AXES)
    blocks = lax.axis_size(ROW_AXES)
    rows, columns = queries.shape
    width = columns // groups
    kv = exchange(split(groups, keys, values), HEAD_AXES)
    kv = lax.all_gather(kv, KEY_AXES, axis=0, tiled=True)
    q = exchange(split(groups, queries), HEAD_AXES).reshape(1, groups * rows, width)
    q = exchange(jnp.broadcast_to(q, (blocks, groups * rows, width)), ROW_AXES)
    steps = (2, 1, 3, 0)
    place = lax.axis_index(ROW_AXES)
    at = jnp.stack([lax.rem(place + step, blocks) for step in steps]).astype(jnp.int32)
    parts = [
        lax.ppermute(part, ROW_AXES, [(i, (i + step) % blocks) for i in range(blocks)])
        if step
        else part
        for step, part in zip(steps, attend(at, q, kv))
    ]
    merged = merge(parts).reshape(groups, rows, width)
    spread = exchange(merged, HEAD_AXES)
    return spread.transpose(1, 0, 2).reshape(rows, columns)


def solution(mesh):
    fine = Mesh(mesh.devices.reshape(4, 2, 8, 4, 2), ALL_AXES)
    placed = P(ALL_AXES, None)
    return jax.shard_map(
        shards, mesh=fine, in_specs=(placed,) * 3, out_specs=placed, check_vma=False
    )
```

time: 142 us -> 148 us (1.042)
  blocking collectives: 83.4 us -> 55.1 us
  waiting for transfers between devices: 16.7 us -> 31.9 us
  starting transfers between devices: 1.91 us -> 14 us
  Pallas kernels: 22.1 us -> 29.7 us
    all_to_all x5 -> x3, blocking collectives: 83.4 us -> 55.1 us  [exchange(): return lax.all_to_all(array, axes, split_axis=0, concat_axis=0, tiled=True)]
    ppermute x1 -> x3, waiting for transfers between devices: 0.01 us -> 8.14 us  [shards(): lax.ppermute(part, ROW_AXES, [(i, (i + step) % blocks) for i in range(blo...]
    pallas_call x2 -> x1, Pallas kernels: 18.1 us -> 25.7 us  [attend(): pl.pallas_call(attend_kernel, in_specs=[pl.BlockSpec(memory_space=pltpu.S...]
    ppermute x1 -> x3, starting transfers between devices: 1.91 us -> 9.26 us  [shards(): lax.ppermute(part, ROW_AXES, [(i, (i + step) % blocks) for i in range(blo...]
    all_to_all x0 -> x1, waiting for transfers between devices: none -> 7.05 us  [exchange(): return lax.all_to_all(array, axes, split_axis=0, concat_axis=0, tiled=True)]
    all_to_all x0 -> x1, starting transfers between devices: none -> 4.77 us  [exchange(): return lax.all_to_all(array, axes, split_axis=0, concat_axis=0, tiled=True)]
  transfers between devices with their start and end apart: 2 -> 5, of which waited for: 1 -> 5; matrix products, arithmetic and copies ran while one was open for 0% -> 1% of each run, Pallas kernels for 7% -> 1%
where the time goes in v5:
time: 148 us; the launch traced here: 147 us
  blocking collectives  55.1 us (37%)
  waiting for transfers between devices  31.9 us (22%)
  Pallas kernels  29.7 us (20%)
  starting transfers between devices  14 us (9%)
  between operations  13.4 us (9%)
  local copies, waits for them, and re-layouts  2.61 us (2%)
    all_to_all x3, blocking collectives, exchange(): return lax.all_to_all(array, axes, split_axis=0, concat_axis=0, tiled=True)  55.1 us
    pallas_call x1, Pallas kernels, attend(): pl.pallas_call(attend_kernel, in_specs=[pl.BlockSpec(memory_space=pltpu.S...  25.7 us
    all_gather x1, waiting for transfers between devices, shards(): kv = lax.all_gather(kv, KEY_AXES, axis=0, tiled=True)  16.7 us
    ppermute x3, starting transfers between devices, shards(): lax.ppermute(part, ROW_AXES, [(i, (i + step) % blocks) for i in range(blo...  9.26 us
    ppermute x3, waiting for transfers between devices, shards(): lax.ppermute(part, ROW_AXES, [(i, (i + step) % blocks) for i in range(blo...  8.14 us
    all_to_all x1, waiting for transfers between devices, exchange(): return lax.all_to_all(array, axes, split_axis=0, concat_axis=0, tiled=True)  7.05 us
    all_to_all x1, starting transfers between devices, exchange(): return lax.all_to_all(array, axes, split_axis=0, concat_axis=0, tiled=True)  4.77 us
    pallas_call x2, Pallas kernels, split(): pl.pallas_call(split_kernel, out_shape=jax.ShapeDtypeStruct((groups, len(...  3.43 us
  transfers between devices with their start and end apart: 5, of which 5 were waited for; matrix products, arithmetic and copies ran while one was open for 1% of the time, Pallas kernels for 1%

profile of v5, /device:TPU:6, one launch (start us, length us, event | category | flops | bytes accessed | tf_op | source)
XLA Modules:
  0.0 147.4 jit_solution(11443489093430149933)
XLA Ops:
  6.5 0.0 all-gather.2.cloned.1.call-start
  6.5 1.8 %shard_map.38 = bf16[8,2,32,384]{3,2,1,0:T(8,128)(2,1)} custom-call(bf16[32,3072]{1,0:T(8,128)(2,1)} %refs_0_.3, bf16[32,3072]{1,0:T(8,128)(2,1)} %refs_1_.1), custom_call_target="tpu_custom_call" | custom-call | tf_op jit(solution)/shard_map/pallas_call | solution.py:185
  8.3 25.1 %all_to_all.20 = bf16[8,2,32,384]{3,2,1,0:T(8,128)(2,1)} all-to-all(bf16[8,2,32,384]{3,2,1,0:T(8,128)(2,1)} %shard_map.38), channel_id=1, replica_groups=mesh['x'=4,'zl'=2,'y'=8,'zh'=4,'c'=2] {'zh','zl'}, dimensions={0} | all-to-all | bytes 786432 | tf_op jit(solution)/shard_map/all_to_all | solution.py:202
  33.4 0.0 all-gather.2.cloned.1.call-update
  33.5 1.6 %shard_map.37 = bf16[8,1,32,384]{3,2,1,0:T(8,128)(2,1)} custom-call(bf16[32,3072]{1,0:T(8,128)(2,1)} %refs_0_.2), custom_call_target="tpu_custom_call" | custom-call | tf_op jit(solution)/shard_map/pallas_call | solution.py:185
  35.1 13.1 %all_to_all.21 = bf16[8,1,32,384]{3,2,1,0:T(8,128)(2,1)S(1)} all-to-all(bf16[8,1,32,384]{3,2,1,0:T(8,128)(2,1)} %shard_map.37), channel_id=1, replica_groups=mesh['x'=4,'zl'=2,'y'=8,'zh'=4,'c'=2] {'zh','zl'}, dimensions={0} | all-to-all | bytes 393216 | tf_op jit(solution)/shard_map/all_to_all | solution.py:202
  48.2 1.0 broadcast_in_dim.8
  49.1 4.8 %all-to-all-start.1 = ((bf16[4,256,384]{2,1,0:T(8,128)(2,1)}), bf16[4,256,384]{2,1,0:T(8,128)(2,1)S(1)}, u32[]{:S(2)}, u32[]{:S(2)}) async-start(bf16[4,256,384]{2,1,0:T(8,128)(2,1)} %broadcast_in_dim.8), calls=%async_computation.1 | async-start | bytes 1572864 | tf_op jit(solution)/shard_map/all_to_all | solution.py:202
  53.9 0.6 pad_add_fusion.at_ref
  54.5 7.1 %all-to-all-done.1.q_ref = bf16[4,256,384]{2,1,0:T(8,128)(2,1)S(1)} async-done(((bf16[4,256,384]{2,1,0:T(8,128)(2,1)}), bf16[4,256,384]{2,1,0:T(8,128)(2,1)S(1)}, u32[]{:S(2)}, u32[]{:S(2)}) %all-to-all-start.1) | async-done | bytes 786464 | tf_op jit(solution)/shard_map/all_to_all | solution.py:202
  61.6 0.0 copy-start.1
  61.6 16.7 %all-gather.2.cloned.1.call-done.kv_ref = bf16[128,2,32,384]{3,2,1,0:T(8,128)(2,1)} async-done(((bf16[8,2,32,384]{3,2,1,0:T(8,128)(2,1)}), bf16[128,2,32,384]{3,2,1,0:T(8,128)(2,1)}) %all-gather.2.cloned.1.call-update) | async-done | bytes 6291472 | tf_op jit(solution)/shard_map/all_gather | solution.py:211
  78.2 0.0 copy-done.1
  78.2 25.7 %shard_map.39 = (bf16[272,384]{1,0:T(8,128)(2,1)}, bf16[272,384]{1,0:T(8,128)(2,1)}, bf16[272,384]{1,0:T(8,128)(2,1)}, bf16[272,384]{1,0:T(8,128)(2,1)}) custom-call(s32[4]{0:T(128)} %pad_add_fusion.at_ref, bf16[4,256,384]{2,1,0:T(8,128)(2,1)} %copy-done.1, bf16[128,2,32,384]{3,2,1,0:T(8,128)(2,1)} %all-gather.2.cloned.1.call-done.kv_ref), custom_call_target="tpu_custom_call" | custom-call | flops 6442450944 | bytes 7864320 | tf_op jit(solution)/shard_map/pallas_call | solution.py:117
  103.9 3.4 %collective-permute-start = (bf16[272,384]{1,0:T(8,128)(2,1)}, bf16[272,384]{1,0:T(8,128)(2,1)S(1)}, u32[]{:S(2)}, u32[]{:S(2)}) collective-permute-start(bf16[272,384]{1,0:T(8,128)(2,1)} %get-tuple-element.9), channel_id=1, source_target_pairs={{0,256},{128,384},{256,0},{384,128},{1,257},{129,385},{257,1},{385... | collective-permute-start | bytes 626696 | tf_op jit(solution)/shard_map/ppermute | solution.py:218
  107.3 4.0 %collective-permute-start.1 = (bf16[272,384]{1,0:T(8,128)(2,1)}, bf16[272,384]{1,0:T(8,128)(2,1)S(1)}, u32[]{:S(2)}, u32[]{:S(2)}) collective-permute-start(bf16[272,384]{1,0:T(8,128)(2,1)} %get-tuple-element.10), channel_id=1, source_target_pairs={{0,128},{128,256},{256,384},{384,0},{1,129},{129,257},{257,385},{3... | collective-permute-start | bytes 626696 | tf_op jit(solution)/shard_map/ppermute | solution.py:218
  111.3 1.9 %collective-permute-start.2 = (bf16[272,384]{1,0:T(8,128)(2,1)}, bf16[272,384]{1,0:T(8,128)(2,1)S(1)}, u32[]{:S(2)}, u32[]{:S(2)}) collective-permute-start(bf16[272,384]{1,0:T(8,128)(2,1)} %get-tuple-element.11), channel_id=1, source_target_pairs={{0,384},{128,0},{256,128},{384,256},{1,385},{129,1},{257,129},{385... | collective-permute-start | bytes 626696 | tf_op jit(solution)/shard_map/ppermute | solution.py:218
  113.2 1.6 %collective-permute-done.refs_0_ = bf16[272,384]{1,0:T(8,128)(2,1)S(1)} collective-permute-done((bf16[272,384]{1,0:T(8,128)(2,1)}, bf16[272,384]{1,0:T(8,128)(2,1)S(1)}, u32[]{:S(2)}, u32[]{:S(2)}) %collective-permute-start) | collective-permute-done | bytes 208928 | tf_op jit(solution)/shard_map/ppermute | solution.py:218
  114.9 2.3 %collective-permute-done.1.refs_1_ = bf16[272,384]{1,0:T(8,128)(2,1)S(1)} collective-permute-done((bf16[272,384]{1,0:T(8,128)(2,1)}, bf16[272,384]{1,0:T(8,128)(2,1)S(1)}, u32[]{:S(2)}, u32[]{:S(2)}) %collective-permute-start.1) | collective-permute-done | bytes 208928 | tf_op jit(solution)/shard_map/ppermute | solution.py:218
  117.2 4.2 %collective-permute-done.2.refs_2_ = bf16[272,384]{1,0:T(8,128)(2,1)S(1)} collective-permute-done((bf16[272,384]{1,0:T(8,128)(2,1)}, bf16[272,384]{1,0:T(8,128)(2,1)S(1)}, u32[]{:S(2)}, u32[]{:S(2)}) %collective-permute-start.2) | collective-permute-done | bytes 208928 | tf_op jit(solution)/shard_map/ppermute | solution.py:218
  121.4 0.0 copy-start
  121.4 0.9 copy-done
  122.3 0.6 shard_map.40
  122.9 17.0 %all_to_all.22 = bf16[8,32,384]{2,1,0:T(8,128)(2,1)S(1)} all-to-all(bf16[8,32,384]{2,1,0:T(8,128)(2,1)S(1)} %bitcast.9), channel_id=1, replica_groups=mesh['x'=4,'zl'=2,'y'=8,'zh'=4,'c'=2] {'zh','zl'}, dimensions={0} | all-to-all | bytes 393216 | tf_op jit(solution)/shard_map/all_to_all | solution.py:202
  139.9 0.7 copy.6
Async XLA Ops:
  6.5 71.7 %all-gather.2.cloned.1.call-start = ((), (), s32[]{:S(2)}) async-start(), calls=%async_computation.4 | async-start | bytes 6684672 | tf_op jit(solution)/shard_map/all_gather | solution.py:211
  49.1 12.4 %all-to-all-start.1 = ((bf16[4,256,384]{2,1,0:T(8,128)(2,1)}), bf16[4,256,384]{2,1,0:T(8,128)(2,1)S(1)}, u32[]{:S(2)}, u32[]{:S(2)}) async-start(bf16[4,256,384]{2,1,0:T(8,128)(2,1)} %broadcast_in_dim.8), calls=%async_computation.1 | async-start | bytes 1572864 | tf_op jit(solution)/shard_map/all_to_all | solution.py:202
  61.6 16.7 %copy-start.1 = (bf16[4,256,384]{2,1,0:T(8,128)(2,1)}, bf16[4,256,384]{2,1,0:T(8,128)(2,1)S(1)}, u32[]{:S(2)}) copy-start(bf16[4,256,384]{2,1,0:T(8,128)(2,1)S(1)} %all-to-all-done.1.q_ref) | copy-start | bytes 2359300
  103.9 10.9 %collective-permute-start = (bf16[272,384]{1,0:T(8,128)(2,1)}, bf16[272,384]{1,0:T(8,128)(2,1)S(1)}, u32[]{:S(2)}, u32[]{:S(2)}) collective-permute-start(bf16[272,384]{1,0:T(8,128)(2,1)} %get-tuple-element.9), channel_id=1, source_target_pairs={{0,256},{128,384},{256,0},{384,128},{1,257},{129,385},{257,1},{385... | collective-permute-start | bytes 626696 | tf_op jit(solution)/shard_map/ppermute | solution.py:218
  107.3 9.9 %collective-permute-start.1 = (bf16[272,384]{1,0:T(8,128)(2,1)}, bf16[272,384]{1,0:T(8,128)(2,1)S(1)}, u32[]{:S(2)}, u32[]{:S(2)}) collective-permute-start(bf16[272,384]{1,0:T(8,128)(2,1)} %get-tuple-element.10), channel_id=1, source_target_pairs={{0,128},{128,256},{256,384},{384,0},{1,129},{129,257},{257,385},{3... | collective-permute-start | bytes 626696 | tf_op jit(solution)/shard_map/ppermute | solution.py:218
  111.3 10.1 %collective-permute-start.2 = (bf16[272,384]{1,0:T(8,128)(2,1)}, bf16[272,384]{1,0:T(8,128)(2,1)S(1)}, u32[]{:S(2)}, u32[]{:S(2)}) collective-permute-start(bf16[272,384]{1,0:T(8,128)(2,1)} %get-tuple-element.11), channel_id=1, source_target_pairs={{0,384},{128,0},{256,128},{384,256},{1,385},{129,1},{257,129},{385... | collective-permute-start | bytes 626696 | tf_op jit(solution)/shard_map/ppermute | solution.py:218
  121.4 0.9 copy-start
Sparse Core Ops, SparseCore 0:
  33.6 44.6 all-gather.1

commit v6 on v5

v6 whole, which is shorter than its diff:
```python
import functools
import math

import jax
import jax.numpy as jnp
from jax import lax
from jax.experimental import pallas as pl
from jax.experimental.pallas import tpu as pltpu
from jax.sharding import Mesh, PartitionSpec as P

HEAD_DIM = 128
STAT_ROWS = 16
KEY_CHUNK = 512
EXPONENT = HEAD_DIM**-0.5 * math.log2(math.e)


def head_cols(h):
    return slice(h * HEAD_DIM, (h + 1) * HEAD_DIM)


def attend_kernel(q_ref, kv_ref, out_ref, held_ref, copied, score_a, score_b):
    score_refs = (score_a, score_b)
    blocks, rows, width = q_ref.shape
    heads = width // HEAD_DIM
    unit_rows = score_a.shape[0]
    per_unit = unit_rows // rows
    units = blocks // per_unit
    run = held_ref.shape[2]
    step = KEY_CHUNK // run
    chunks = held_ref.shape[0] // (2 * step)

    def copy(j):
        part = pl.ds(j * step, step)
        return pltpu.make_async_copy(kv_ref.at[part], held_ref.at[part], copied.at[j])

    def kv_chunk(which, h, j):
        block = held_ref[j * step : (j + 1) * step, which, :, head_cols(h)]
        return block.reshape(KEY_CHUNK, HEAD_DIM)

    def query(i, h):
        block = q_ref[pl.ds(i * per_unit, per_unit), :, head_cols(h)]
        return block.reshape(unit_rows, HEAD_DIM)

    def cols_of(j):
        return slice(j * KEY_CHUNK, (j + 1) * KEY_CHUNK)

    def score_chunk(q, h, half, slot, j, top):
        k = kv_chunk(0, h, half * chunks + j)
        s = lax.dot_general(q, k, (((1,), (1,)), ((), ())), preferred_element_type=jnp.float32)
        score_refs[slot][:, cols_of(j)] = s
        for t in range(KEY_CHUNK // HEAD_DIM):
            part = s[:, head_cols(t)]
            top = part if top is None else jnp.maximum(top, part)
        return top

    def shift_of(top):
        best = jnp.max(top, axis=1, keepdims=True) * EXPONENT
        return best.astype(jnp.bfloat16).astype(jnp.float32)

    for j in range(2 * chunks):
        copy(j).start()
    ones = jnp.ones((KEY_CHUNK, HEAD_DIM), jnp.bfloat16)
    order = [(half, h) for half in range(2) for h in range(heads)]
    top = None
    q = query(0, 0)
    for j in range(chunks):
        copy(j).wait()
        top = score_chunk(q, 0, 0, 0, j, top)

    def rows_step(i, shift):
        lane = lax.broadcasted_iota(jnp.int32, (unit_rows, HEAD_DIM), 1)
        stats = jnp.zeros((unit_rows, HEAD_DIM), jnp.float32)
        held = {}
        for n, (half, h) in enumerate(order):
            if n == heads - 1:

                @pl.when(i == 0)
                def _():
                    for j in range(chunks, 2 * chunks):
                        copy(j).wait()

            wraps = n + 1 == len(order)
            next_half, next_h = order[(n + 1) % len(order)]
            q = query(jnp.minimum(i + 1, units - 1) if wraps else i, next_h)
            if half:
                shift_before, total_before = held[h]
                shift = jnp.maximum(shift, shift_before)
            top, total = None, None
            for j in range(chunks):
                top = score_chunk(q, next_h, next_half, (n + 1) % 2, j, top)
                s = score_refs[n % 2][:, cols_of(j)]
                e = jnp.exp2(s * EXPONENT - shift).astype(jnp.bfloat16)
                v = jnp.concatenate([kv_chunk(1, h, half * chunks + j), ones], axis=1)
                o = jnp.dot(e, v, preferred_element_type=jnp.float32)
                total = o if total is None else total + o
            if half:
                total = total + jnp.exp2(shift_before - shift) * total_before
                for b in range(per_unit):
                    part = total[b * rows : (b + 1) * rows, 0:HEAD_DIM].astype(jnp.bfloat16)
                    out_ref[i * per_unit + b, 0:rows, head_cols(h)] = part
                denom = total[:, HEAD_DIM:]
                high = denom.astype(jnp.bfloat16).astype(jnp.float32)
                stats = jnp.where(lane == h, shift, stats)
                stats = jnp.where(lane == heads + h, high, stats)
                stats = jnp.where(lane == 2 * heads + h, denom - high, stats)
            else:
                held[h] = shift, total
            shift = shift_of(top)
        flipped = stats.T[0:STAT_ROWS].astype(jnp.bfloat16)
        blank = jnp.zeros((STAT_ROWS, width - rows), jnp.bfloat16)
        for b in range(per_unit):
            block = i * per_unit + b
            out_ref[block, rows:, 0:rows] = flipped[:, b * rows : (b + 1) * rows]
            out_ref[block, rows:, rows:] = blank
        return shift

    lax.fori_loop(0, units, rows_step, shift_of(top))


def attend(q, kv):
    blocks, rows, width = q.shape
    heads = width // HEAD_DIM
    keys_n = kv.shape[0] * kv.shape[2]
    vmem = pl.BlockSpec(memory_space=pltpu.VMEM)
    unit_rows = 2 * rows
    return pl.pallas_call(
        attend_kernel,
        in_specs=[vmem, pl.BlockSpec(memory_space=pl.ANY)],
        out_specs=vmem,
        out_shape=jax.ShapeDtypeStruct((blocks, rows + STAT_ROWS, width), jnp.bfloat16),
        scratch_shapes=[
            pltpu.VMEM(kv.shape, kv.dtype),
            pltpu.SemaphoreType.DMA((keys_n // KEY_CHUNK,)),
            pltpu.VMEM((unit_rows, keys_n // 2), jnp.float32),
            pltpu.VMEM((unit_rows, keys_n // 2), jnp.float32),
        ],
        compiler_params=pltpu.CompilerParams(vmem_limit_bytes=56 * 2**20),
        cost_estimate=pl.CostEstimate(
            flops=4 * blocks * rows * keys_n * width,
            bytes_accessed=4 * (blocks * rows * width + keys_n * width),
            transcendentals=blocks * rows * keys_n * heads,
        ),
    )(q, kv)


def merge_kernel(parts_ref, out_ref):
    pieces = parts_ref.shape[0]
    rows, width = out_ref.shape
    heads = width // HEAD_DIM
    stats = [
        parts_ref[p, rows : rows + STAT_ROWS, 0:rows].astype(jnp.float32) for p in range(pieces)
    ]
    shifts = [s[0:heads] for s in stats]
    totals = [s[heads : 2 * heads] + s[2 * heads : 3 * heads] for s in stats]
    best = functools.reduce(jnp.maximum, shifts)
    factors = [jnp.exp2(s - best) for s in shifts]
    denom = sum(f * t for f, t in zip(factors, totals))
    weights = jnp.concatenate([f / denom for f in factors], axis=0)
    pad = jnp.zeros((HEAD_DIM - weights.shape[0], rows), jnp.float32)
    weights = jnp.concatenate([weights, pad], axis=0).T
    for h in range(heads):
        total = jnp.zeros((rows, HEAD_DIM), jnp.float32)
        for p in range(pieces):
            w = weights[:, p * heads + h : p * heads + h + 1]
            total = total + w * parts_ref[p, 0:rows, head_cols(h)].astype(jnp.float32)
        out_ref[:, head_cols(h)] = total.astype(jnp.bfloat16)


def merge(parts):
    pieces, part_rows, width = parts.shape
    return pl.pallas_call(
        merge_kernel,
        out_shape=jax.ShapeDtypeStruct((part_rows - STAT_ROWS, width), jnp.bfloat16),
        in_specs=[pl.BlockSpec(memory_space=pltpu.VMEM)],
        out_specs=pl.BlockSpec(memory_space=pltpu.VMEM),
        compiler_params=pltpu.CompilerParams(vmem_limit_bytes=32 * 2**20),
    )(parts)


def split_kernel(*refs):
    *in_refs, out_ref = refs
    groups, arrays, rows, width = out_ref.shape
    for g in range(groups):
        for a in range(arrays):
            out_ref[g, a] = in_refs[a][:, g * width : (g + 1) * width]


def split(groups, *arrays):
    rows, columns = arrays[0].shape
    return pl.pallas_call(
        split_kernel,
        out_shape=jax.ShapeDtypeStruct(
            (groups, len(arrays), rows, columns // groups), arrays[0].dtype
        ),
        in_specs=[pl.BlockSpec(memory_space=pltpu.VMEM)] * len(arrays),
        out_specs=pl.BlockSpec(memory_space=pltpu.VMEM),
    )(*arrays)


HEAD_AXES = ("zh", "zl")
KEY_AXES = ("y", "c")
ROW_AXES = ("x",)
ALL_AXES = ("x", "zl", "y", "zh", "c")


def exchange(array, axes):
    return lax.all_to_all(array, axes, split_axis=0, concat_axis=0, tiled=True)


def shards(queries, keys, values):
    groups = lax.axis_size(HEAD_AXES)
    blocks = lax.axis_size(ROW_AXES)
    rows, columns = queries.shape
    width = columns // groups
    kv = exchange(split(groups, keys, values), HEAD_AXES)
    kv = lax.all_gather(kv, KEY_AXES, axis=0, tiled=True)
    q = exchange(split(groups, queries), HEAD_AXES).reshape(1, groups * rows, width)
    q = exchange(jnp.broadcast_to(q, (blocks, groups * rows, width)), ROW_AXES)
    parts = attend(q, kv)
    merged = merge(exchange(parts, ROW_AXES)).reshape(groups, rows, width)
    spread = exchange(merged, HEAD_AXES)
    return spread.transpose(1, 0, 2).reshape(rows, columns)


def solution(mesh):
    fine = Mesh(mesh.devices.reshape(4, 2, 8, 4, 2), ALL_AXES)
    placed = P(ALL_AXES, None)
    return jax.shard_map(
        shards, mesh=fine, in_specs=(placed,) * 3, out_specs=placed, check_vma=False
    )
```

time: 148 us -> 140 us (0.946)
  blocking collectives: 55.1 us -> 83.4 us
  waiting for transfers between devices: 31.9 us -> 17.7 us
  starting transfers between devices: 14 us -> 0.01 us
  Pallas kernels: 29.7 us -> 23.1 us
  local copies, waits for them, and re-layouts: 2.61 us -> 0.77 us
    all_to_all x3 -> x5, blocking collectives: 55.1 us -> 83.4 us  [exchange(): return lax.all_to_all(array, axes, split_axis=0, concat_axis=0, tiled=True)]
    ppermute x3 -> x0, starting transfers between devices: 9.26 us -> none  [shards(): lax.ppermute(part, ROW_AXES, [(i, (i + step) % blocks) for i in range(blo...]
    ppermute x3 -> x0, waiting for transfers between devices: 8.14 us -> none  [shards(): lax.ppermute(part, ROW_AXES, [(i, (i + step) % blocks) for i in range(blo...]
    all_to_all x1 -> x0, waiting for transfers between devices: 7.05 us -> none  [exchange(): return lax.all_to_all(array, axes, split_axis=0, concat_axis=0, tiled=True)]
    pallas_call x1, Pallas kernels: 25.7 us -> 19.1 us  [attend(): pl.pallas_call(attend_kernel, in_specs=[vmem, pl.BlockSpec(memory_space=p...]
    all_to_all x1 -> x0, starting transfers between devices: 4.77 us -> none  [exchange(): return lax.all_to_all(array, axes, split_axis=0, concat_axis=0, tiled=True)]
  transfers between devices with their start and end apart: 5 -> 1, of which waited for: 5 -> 1; matrix products, arithmetic and copies ran while one was open for 1% -> 0% of each run, Pallas kernels for 1% -> 1%
where the time goes in v6:
time: 140 us; the launch traced here: 138 us
  blocking collectives  83.4 us (60%)
  Pallas kernels  23.1 us (16%)
  waiting for transfers between devices  17.7 us (13%)
  between operations  13.4 us (10%)
    all_to_all x5, blocking collectives, exchange(): return lax.all_to_all(array, axes, split_axis=0, concat_axis=0, tiled=True)  83.4 us
    pallas_call x1, Pallas kernels, attend(): pl.pallas_call(attend_kernel, in_specs=[vmem, pl.BlockSpec(memory_space=p...  19.1 us
    all_gather x1, waiting for transfers between devices, shards(): kv = lax.all_gather(kv, KEY_AXES, axis=0, tiled=True)  17.7 us
    pallas_call x2, Pallas kernels, split(): pl.pallas_call(split_kernel, out_shape=jax.ShapeDtypeStruct((groups, len(...  3.43 us
  transfers between devices with their start and end apart: 1, of which 1 were waited for; matrix products, arithmetic and copies ran while one was open for 0% of the time, Pallas kernels for 1%

profile of v6, /device:TPU:6, one launch (start us, length us, event | category | flops | bytes accessed | tf_op | source)
XLA Modules:
  0.0 138.4 jit_solution(10047552022733284581)
XLA Ops:
  6.5 0.0 all-gather.2.cloned.1.call-start
  6.5 1.8 %shard_map.38 = bf16[8,2,32,384]{3,2,1,0:T(8,128)(2,1)} custom-call(bf16[32,3072]{1,0:T(8,128)(2,1)} %refs_0_.3, bf16[32,3072]{1,0:T(8,128)(2,1)} %refs_1_.1), custom_call_target="tpu_custom_call" | custom-call | tf_op jit(solution)/shard_map/pallas_call | solution.py:190
  8.3 25.1 %all_to_all.25 = bf16[8,2,32,384]{3,2,1,0:T(8,128)(2,1)} all-to-all(bf16[8,2,32,384]{3,2,1,0:T(8,128)(2,1)} %shard_map.38), channel_id=1, replica_groups=mesh['x'=4,'zl'=2,'y'=8,'zh'=4,'c'=2] {'zh','zl'}, dimensions={0} | all-to-all | bytes 786432 | tf_op jit(solution)/shard_map/all_to_all | solution.py:207
  33.5 0.0 all-gather.2.cloned.1.call-update
  33.5 1.6 %shard_map.37 = bf16[8,1,32,384]{3,2,1,0:T(8,128)(2,1)} custom-call(bf16[32,3072]{1,0:T(8,128)(2,1)} %refs_0_.2), custom_call_target="tpu_custom_call" | custom-call | tf_op jit(solution)/shard_map/pallas_call | solution.py:190
  35.1 13.1 %all_to_all.26 = bf16[8,1,32,384]{3,2,1,0:T(8,128)(2,1)S(1)} all-to-all(bf16[8,1,32,384]{3,2,1,0:T(8,128)(2,1)} %shard_map.37), channel_id=1, replica_groups=mesh['x'=4,'zl'=2,'y'=8,'zh'=4,'c'=2] {'zh','zl'}, dimensions={0} | all-to-all | bytes 393216 | tf_op jit(solution)/shard_map/all_to_all | solution.py:207
  48.2 0.1 broadcast_in_dim.8
  48.2 12.3 %all_to_all.27.q_ref = bf16[4,256,384]{2,1,0:T(8,128)(2,1)} all-to-all(bf16[4,256,384]{2,1,0:T(8,128)(2,1)S(1)} %broadcast_in_dim.8), channel_id=1, replica_groups=mesh['x'=4,'zl'=2,'y'=8,'zh'=4,'c'=2] {'x'}, dimensions={0} | all-to-all | bytes 1572864 | tf_op jit(solution)/shard_map/all_to_all | solution.py:207
  60.6 17.7 %all-gather.2.cloned.1.call-done.kv_ref = bf16[128,2,32,384]{3,2,1,0:T(8,128)(2,1)} async-done(((bf16[8,2,32,384]{3,2,1,0:T(8,128)(2,1)}), bf16[128,2,32,384]{3,2,1,0:T(8,128)(2,1)}) %all-gather.2.cloned.1.call-update) | async-done | bytes 6291472 | tf_op jit(solution)/shard_map/all_gather | solution.py:216
  78.2 19.1 %shard_map.39 = bf16[4,272,384]{2,1,0:T(8,128)(2,1)} custom-call(bf16[4,256,384]{2,1,0:T(8,128)(2,1)} %all_to_all.27.q_ref, bf16[128,2,32,384]{3,2,1,0:T(8,128)(2,1)} %all-gather.2.cloned.1.call-done.kv_ref), custom_call_target="tpu_custom_call" | custom-call | flops 6442450944 | bytes 7864320 | tf_op jit(solution)/shard_map/pallas_call | solution.py:126
  97.3 16.0 %all_to_all.28.parts_ref = bf16[4,272,384]{2,1,0:T(8,128)(2,1)S(1)} all-to-all(bf16[4,272,384]{2,1,0:T(8,128)(2,1)} %shard_map.39), channel_id=1, replica_groups=mesh['x'=4,'zl'=2,'y'=8,'zh'=4,'c'=2] {'x'}, dimensions={0} | all-to-all | bytes 1671168 | tf_op jit(solution)/shard_map/all_to_all | solution.py:207
  113.3 0.6 shard_map.40
  113.9 17.0 %all_to_all.29 = bf16[8,32,384]{2,1,0:T(8,128)(2,1)S(1)} all-to-all(bf16[8,32,384]{2,1,0:T(8,128)(2,1)S(1)} %bitcast.5), channel_id=1, replica_groups=mesh['x'=4,'zl'=2,'y'=8,'zh'=4,'c'=2] {'zh','zl'}, dimensions={0} | all-to-all | bytes 393216 | tf_op jit(solution)/shard_map/all_to_all | solution.py:207
  130.9 0.7 copy.6
Async XLA Ops:
  6.5 71.7 %all-gather.2.cloned.1.call-start = ((), (), s32[]{:S(2)}) async-start(), calls=%async_computation.5 | async-start | bytes 6684672 | tf_op jit(solution)/shard_map/all_gather | solution.py:216
Sparse Core Ops, SparseCore 0:
  33.6 44.6 all-gather.1

commit v7 on v6

--- a/solution.py
+++ b/solution.py
@@ -85,14 +85,19 @@
             if half:
                 shift_before, total_before = held[h]
                 shift = jnp.maximum(shift, shift_before)
-            top, total = None, None
-            for j in range(chunks):
-                top = score_chunk(q, next_h, next_half, (n + 1) % 2, j, top)
-                s = score_refs[n % 2][:, cols_of(j)]
-                e = jnp.exp2(s * EXPONENT - shift).astype(jnp.bfloat16)
-                v = jnp.concatenate([kv_chunk(1, h, half * chunks + j), ones], axis=1)
-                o = jnp.dot(e, v, preferred_element_type=jnp.float32)
-                total = o if total is None else total + o
+            top, total, waiting = None, None, None
+            for j in range(chunks + 1):
+                if j < chunks:
+                    top = score_chunk(q, next_h, next_half, (n + 1) % 2, j, top)
+                if j == chunks - 1:
+                    shift_after = shift_of(top)
+                if j > 0:
+                    v = jnp.concatenate([kv_chunk(1, h, half * chunks + j - 1), ones], axis=1)
+                    o = jnp.dot(waiting, v, preferred_element_type=jnp.float32)
+                    total = o if total is None else total + o
+                if j < chunks:
+                    s = score_refs[n % 2][:, cols_of(j)]
+                    waiting = jnp.exp2(s * EXPONENT - shift).astype(jnp.bfloat16)
             if half:
                 total = total + jnp.exp2(shift_before - shift) * total_before
                 for b in range(per_unit):
@@ -105,7 +110,7 @@
                 stats = jnp.where(lane == 2 * heads + h, denom - high, stats)
             else:
                 held[h] = shift, total
-            shift = shift_of(top)
+            shift = shift_after
         flipped = stats.T[0:STAT_ROWS].astype(jnp.bfloat16)
         blank = jnp.zeros((STAT_ROWS, width - rows), jnp.bfloat16)
         for b in range(per_unit):

time: 140 us -> 140 us (level)
  no operation moved by 1% of the time
where the time goes in v7:
time: 140 us; the launch traced here: 138 us
  blocking collectives  83.4 us (60%)
  Pallas kernels  23.1 us (16%)
  waiting for transfers between devices  17.7 us (13%)
  between operations  13.4 us (10%)
    all_to_all x5, blocking collectives, exchange(): return lax.all_to_all(array, axes, split_axis=0, concat_axis=0, tiled=True)  83.4 us
    pallas_call x1, Pallas kernels, attend(): pl.pallas_call(attend_kernel, in_specs=[vmem, pl.BlockSpec(memory_space=p...  19.1 us
    all_gather x1, waiting for transfers between devices, shards(): kv = lax.all_gather(kv, KEY_AXES, axis=0, tiled=True)  17.7 us
    pallas_call x2, Pallas kernels, split(): pl.pallas_call(split_kernel, out_shape=jax.ShapeDtypeStruct((groups, len(...  3.43 us
  transfers between devices with their start and end apart: 1, of which 1 were waited for; matrix products, arithmetic and copies ran while one was open for 0% of the time, Pallas kernels for 1%

profile of v7, /device:TPU:6, one launch (start us, length us, event | category | flops | bytes accessed | tf_op | source)
XLA Modules:
  0.0 138.4 jit_solution(16879376846179487981)
XLA Ops:
  6.5 0.0 all-gather.2.cloned.1.call-start
  6.5 1.8 %shard_map.38 = bf16[8,2,32,384]{3,2,1,0:T(8,128)(2,1)} custom-call(bf16[32,3072]{1,0:T(8,128)(2,1)} %refs_0_.3, bf16[32,3072]{1,0:T(8,128)(2,1)} %refs_1_.1), custom_call_target="tpu_custom_call" | custom-call | tf_op jit(solution)/shard_map/pallas_call | solution.py:195
  8.3 25.1 %all_to_all.25 = bf16[8,2,32,384]{3,2,1,0:T(8,128)(2,1)} all-to-all(bf16[8,2,32,384]{3,2,1,0:T(8,128)(2,1)} %shard_map.38), channel_id=1, replica_groups=mesh['x'=4,'zl'=2,'y'=8,'zh'=4,'c'=2] {'zh','zl'}, dimensions={0} | all-to-all | bytes 786432 | tf_op jit(solution)/shard_map/all_to_all | solution.py:212
  33.5 0.0 all-gather.2.cloned.1.call-update
  33.5 1.6 %shard_map.37 = bf16[8,1,32,384]{3,2,1,0:T(8,128)(2,1)} custom-call(bf16[32,3072]{1,0:T(8,128)(2,1)} %refs_0_.2), custom_call_target="tpu_custom_call" | custom-call | tf_op jit(solution)/shard_map/pallas_call | solution.py:195
  35.1 13.1 %all_to_all.26 = bf16[8,1,32,384]{3,2,1,0:T(8,128)(2,1)S(1)} all-to-all(bf16[8,1,32,384]{3,2,1,0:T(8,128)(2,1)} %shard_map.37), channel_id=1, replica_groups=mesh['x'=4,'zl'=2,'y'=8,'zh'=4,'c'=2] {'zh','zl'}, dimensions={0} | all-to-all | bytes 393216 | tf_op jit(solution)/shard_map/all_to_all | solution.py:212
  48.2 0.1 broadcast_in_dim.8
  48.2 12.3 %all_to_all.27.q_ref = bf16[4,256,384]{2,1,0:T(8,128)(2,1)} all-to-all(bf16[4,256,384]{2,1,0:T(8,128)(2,1)S(1)} %broadcast_in_dim.8), channel_id=1, replica_groups=mesh['x'=4,'zl'=2,'y'=8,'zh'=4,'c'=2] {'x'}, dimensions={0} | all-to-all | bytes 1572864 | tf_op jit(solution)/shard_map/all_to_all | solution.py:212
  60.6 17.7 %all-gather.2.cloned.1.call-done.kv_ref = bf16[128,2,32,384]{3,2,1,0:T(8,128)(2,1)} async-done(((bf16[8,2,32,384]{3,2,1,0:T(8,128)(2,1)}), bf16[128,2,32,384]{3,2,1,0:T(8,128)(2,1)}) %all-gather.2.cloned.1.call-update) | async-done | bytes 6291472 | tf_op jit(solution)/shard_map/all_gather | solution.py:221
  78.2 19.1 %shard_map.39 = bf16[4,272,384]{2,1,0:T(8,128)(2,1)} custom-call(bf16[4,256,384]{2,1,0:T(8,128)(2,1)} %all_to_all.27.q_ref, bf16[128,2,32,384]{3,2,1,0:T(8,128)(2,1)} %all-gather.2.cloned.1.call-done.kv_ref), custom_call_target="tpu_custom_call" | custom-call | flops 6442450944 | bytes 7864320 | tf_op jit(solution)/shard_map/pallas_call | solution.py:131
  97.3 16.0 %all_to_all.28.parts_ref = bf16[4,272,384]{2,1,0:T(8,128)(2,1)S(1)} all-to-all(bf16[4,272,384]{2,1,0:T(8,128)(2,1)} %shard_map.39), channel_id=1, replica_groups=mesh['x'=4,'zl'=2,'y'=8,'zh'=4,'c'=2] {'x'}, dimensions={0} | all-to-all | bytes 1671168 | tf_op jit(solution)/shard_map/all_to_all | solution.py:212
  113.3 0.6 shard_map.40
  113.9 17.0 %all_to_all.29 = bf16[8,32,384]{2,1,0:T(8,128)(2,1)S(1)} all-to-all(bf16[8,32,384]{2,1,0:T(8,128)(2,1)S(1)} %bitcast.5), channel_id=1, replica_groups=mesh['x'=4,'zl'=2,'y'=8,'zh'=4,'c'=2] {'zh','zl'}, dimensions={0} | all-to-all | bytes 393216 | tf_op jit(solution)/shard_map/all_to_all | solution.py:212
  130.9 0.7 copy.6
Async XLA Ops:
  6.5 71.7 %all-gather.2.cloned.1.call-start = ((), (), s32[]{:S(2)}) async-start(), calls=%async_computation.5 | async-start | bytes 6684672 | tf_op jit(solution)/shard_map/all_gather | solution.py:221
Sparse Core Ops, SparseCore 0:
  33.6 44.6 all-gather.1
